TPU v7x, 32 devices: a whole 2x2x4 slice. The times are simulated.
32 devices in a mesh: dp: 8 (over z, y), mp: 4 (over x, core).
Axes of the slice: x: 2, y: 2, z: 4, core: 2. Of those that a mesh axis runs over, the one named last changes fastest.
Arguments:
- features: bfloat16 [9216, 1024], P('dp'), may hold values from -6 to 6
- stem_weight: bfloat16 [1024, 1024], P(None, 'mp'), may hold values from -0.1875 to 0.1875
- group_gain: float32 [1024], P('mp'), may hold values from 0.1 to 1.9
- group_bias: float32 [1024], P('mp'), may hold values from -3 to 3
- embed_weight: bfloat16 [1024, 768], P('mp'), may hold values from -0.1875 to 0.1875
- first_gain: float32 [768], replicated, may hold values from 0.1 to 1.9
- first_bias: float32 [768], replicated, may hold values from -2 to 2
- project_in: bfloat16 [768, 2304], P(None, 'mp'), may hold values from -0.21875 to 0.21875
- project_out: bfloat16 [768, 768], P('mp'), may hold values from -3 to 3
- second_gain: float32 [768], replicated, may hold values from 0.1 to 1.9
- second_bias: float32 [768], replicated, may hold values from -2 to 2
- up_weight: bfloat16 [768, 3072], P(None, 'mp'), may hold values from -0.21875 to 0.21875
- up_bias: float32 [3072], P('mp'), may hold values from -3 to 3
- down_weight: bfloat16 [3072, 768], P('mp'), may hold values from -0.109375 to 0.109375
- valid_mask: int32 [16, 576], replicated, may hold values from 0 to 1, as said below
- slot_slice: int32 [16], P('dp'), may hold values from 0 to 15, each once
- cotangent: bfloat16 [9216, 768], P(('dp', 'mp')), may hold values from -6 to 6
Outputs:
- block_out: bfloat16 [9216, 768], P(('dp', 'mp'))
- features_grad: float32 [9216, 1024], P(('dp', 'mp'))
- stem_weight_grad: float32 [1024, 1024], P(None, 'mp')
- group_gain_grad: float32 [1024], P('mp')
- group_bias_grad: float32 [1024], P('mp')
- embed_weight_grad: float32 [1024, 768], P('mp')
- first_gain_grad: float32 [768], replicated
- first_bias_grad: float32 [768], replicated
- project_in_grad: float32 [768, 2304], P(None, 'mp')
- project_out_grad: float32 [768, 768], P('mp')
- second_gain_grad: float32 [768], replicated
- second_bias_grad: float32 [768], replicated
- up_weight_grad: float32 [768, 3072], P(None, 'mp')
- up_bias_grad: float32 [3072], P('mp')
- down_weight_grad: float32 [3072, 768], P('mp')
Inputs may be any that keep to these rules, and one draw needn't show every extreme that they name: `valid_mask`: row s is 1 at the positions below slice s's valid length, 196 or 576, and 0 after; half of the slices have each length. `slot_slice`: each slice stands in exactly one slot; slots j * 2 to (j + 1) * 2 - 1 are on index j of dp.
All inputs are finite; a program needn't handle non-finite values.
Results may differ from a plain program's by a relative error of at most 0.019.
Values may be sent and summed in bfloat16 or wider, within the bound.
A program may use at most 128 MiB of HBM per device.

v0:
```python
import jax
import jax.numpy as jnp
from jax import lax
from jax.sharding import PartitionSpec as P

HEAD_DIM = 64
CIN = 1024
GROUPS = 32


def gelu_exact(values):
    return jax.nn.gelu(values, approximate=False)


def layer_norm(values, norm_gain, norm_bias):
    average = jnp.mean(values, axis=-1, keepdims=True)
    centered = values - average
    variance = jnp.mean(centered * centered, axis=-1, keepdims=True)
    return centered * lax.rsqrt(variance + 1e-06) * norm_gain + norm_bias


def standardize(matrix):
    average = jnp.mean(matrix, axis=0, keepdims=True)
    centered = matrix - average
    variance = jnp.mean(centered * centered, axis=0, keepdims=True)
    return centered * lax.rsqrt(variance + 1e-05)


def group_norm(stem_out, valid, norm_gain, norm_bias):
    slices, length, channels = stem_out.shape
    group_size = CIN // GROUPS
    grouped = stem_out.reshape(slices, length, channels // group_size, group_size)
    weight = valid[:, :, None, None]
    counted = jnp.sum(valid, axis=1)[:, None, None, None] * group_size
    average = jnp.sum(grouped * weight, axis=(1, 3), keepdims=True) / counted
    centered = grouped - average
    variance = jnp.sum(centered * centered * weight, axis=(1, 3), keepdims=True) / counted
    normed = (centered * lax.rsqrt(variance + 1e-05)).reshape(slices, length, channels)
    return normed * norm_gain + norm_bias


def contract_rows(left, right):
    return lax.dot_general(
        left, right, (((0,), (0,)), ((), ())), preferred_element_type=jnp.float32
    )


def times_transposed(left, right):
    return lax.dot_general(
        left, right, (((1,), (1,)), ((), ())), preferred_element_type=jnp.float32
    )


def plain_or_transposed(left, right, transposed):
    if transposed:
        return times_transposed(left, right)
    return jnp.dot(left, right, preferred_element_type=jnp.float32)


def narrow_product(block_in, weight, transposed):
    return lax.psum_scatter(
        plain_or_transposed(block_in, weight, transposed), "mp", scatter_dimension=0, tiled=True
    )


def slot_scores(queries, key_part, key_valid):
    raw_scores = jnp.einsum("qhd,khd->hqk", queries, key_part, preferred_element_type=jnp.float32)
    scaled = raw_scores * HEAD_DIM ** (-0.5)
    return jnp.where(key_valid[None, None, :] > 0.5, scaled, -1000000000.0)


def attend_slot(slot_in):
    queries, key_part, value_part, key_valid = slot_in
    scores = slot_scores(queries, key_part, key_valid)
    largest = jnp.max(scores, axis=-1, keepdims=True)
    exp_total = jnp.sum(jnp.exp(scores - largest), axis=-1, keepdims=True)
    log_total = largest + jnp.log(exp_total)
    weights = jnp.exp(scores - log_total).astype(jnp.bfloat16)
    mixed_out = jnp.einsum("hqk,khd->qhd", weights, value_part, preferred_element_type=jnp.float32)
    return (mixed_out.astype(jnp.bfloat16), log_total)


def attend_slot_back(slot_in):
    queries, key_part, value_part, key_valid, log_total, mixed_grad = slot_in
    score_scale = HEAD_DIM ** (-0.5)
    probs = jnp.exp(slot_scores(queries, key_part, key_valid) - log_total)
    weights = probs.astype(jnp.bfloat16)
    values_grad = jnp.einsum(
        "hqk,qhd->khd", weights, mixed_grad, preferred_element_type=jnp.float32
    )
    probs_grad = jnp.einsum(
        "qhd,khd->hqk", mixed_grad, value_part, preferred_element_type=jnp.float32
    )
    scores_grad = probs * (probs_grad - jnp.sum(probs * probs_grad, axis=-1, keepdims=True))
    rounded = scores_grad.astype(jnp.bfloat16)
    queries_grad = (
        jnp.einsum("hqk,khd->qhd", rounded, key_part, preferred_element_type=jnp.float32)
        * score_scale
    )
    keys_grad = (
        jnp.einsum("hqk,qhd->khd", rounded, queries, preferred_element_type=jnp.float32)
        * score_scale
    )
    return jnp.stack([queries_grad, keys_grad, values_grad], axis=2)


def sum_feed(up_grad, bias_grad, down_grad):
    return lax.psum((up_grad, bias_grad, down_grad), "dp")


def body(
    features,
    stem_weight,
    group_gain,
    group_bias,
    embed_weight,
    first_gain,
    first_bias,
    project_in,
    project_out,
    second_gain,
    second_bias,
    up_weight,
    up_bias,
    down_weight,
    valid_mask,
    slot_slice,
    cotangent,
):
    mesh_rank = lax.axis_index("mp")
    slices = slot_slice.shape[0]
    tokens = features.shape[0]
    length = tokens // slices
    row_count = cotangent.shape[0]
    slot_valid = jnp.take(valid_mask, slot_slice, axis=0).astype(jnp.float32)
    row_valid = lax.dynamic_slice_in_dim(
        slot_valid.reshape(tokens), mesh_rank * row_count, row_count
    )
    standard, standard_back = jax.vjp(standardize, stem_weight.astype(jnp.float32))
    standard_low = standard.astype(jnp.bfloat16)
    embed_use, out_use, standard_use = (embed_weight, project_out, standard_low)
    stem_out = jnp.dot(features, standard_low, preferred_element_type=jnp.float32)
    channels = stem_out.shape[1]

    def stem_norm(stem_in, gain_in, bias_in):
        normed = group_norm(stem_in.reshape(slices, length, channels), slot_valid, gain_in, bias_in)
        return gelu_exact(normed).reshape(tokens, channels)

    activated, stem_norm_back = jax.vjp(stem_norm, stem_out, group_gain, group_bias)
    activated_low = activated.astype(jnp.bfloat16)
    residual_first = narrow_product(activated_low, embed_use, False)
    normed_one, first_norm_back = jax.vjp(layer_norm, residual_first, first_gain, first_bias)
    normed_one_all = lax.all_gather(normed_one.astype(jnp.bfloat16), "mp", axis=0, tiled=True)
    packed_low = jnp.dot(normed_one_all, project_in, preferred_element_type=jnp.float32).astype(
        jnp.bfloat16
    )
    heads_local = packed_low.shape[1] // (3 * HEAD_DIM)
    packed = packed_low.reshape(slices, length, heads_local, 3, HEAD_DIM)
    queries = packed[:, :, :, 0]
    key_part = packed[:, :, :, 1]
    value_part = packed[:, :, :, 2]
    mixed_out, log_totals = lax.map(attend_slot, (queries, key_part, value_part, slot_valid))
    mixed_flat = mixed_out.reshape(tokens, heads_local * HEAD_DIM)
    residual_second = residual_first + narrow_product(mixed_flat, out_use, False)
    normed_two, second_norm_back = jax.vjp(layer_norm, residual_second, second_gain, second_bias)
    normed_two_all = lax.all_gather(normed_two.astype(jnp.bfloat16), "mp", axis=0, tiled=True)
    hidden_pre = jnp.dot(normed_two_all, up_weight, preferred_element_type=jnp.float32) + up_bias
    hidden, gelu_back = jax.vjp(gelu_exact, hidden_pre)
    hidden_low = hidden.astype(jnp.bfloat16)
    block_in = hidden_low
    residual_third = residual_second + lax.psum_scatter(
        jnp.dot(block_in, down_weight, preferred_element_type=jnp.float32).astype(jnp.bfloat16),
        "mp",
        scatter_dimension=0,
        tiled=True,
    ).astype(jnp.float32)
    block_out = (residual_third * row_valid[:, None]).astype(jnp.bfloat16)
    out_grad = cotangent.astype(jnp.float32) * row_valid[:, None]
    branch_grad = lax.all_gather(out_grad.astype(jnp.bfloat16), "mp", axis=0, tiled=True)
    down_weight_grad = contract_rows(hidden_low, branch_grad)
    hidden_grad = times_transposed(branch_grad, down_weight)
    pre_grad = gelu_back(hidden_grad)[0].astype(jnp.bfloat16)
    up_weight_grad = contract_rows(normed_two_all, pre_grad)
    up_bias_grad = jnp.sum(pre_grad, axis=0, dtype=jnp.float32)
    block_in = pre_grad
    normed_two_grad = lax.psum_scatter(
        times_transposed(block_in, up_weight).astype(jnp.bfloat16),
        "mp",
        scatter_dimension=0,
        tiled=True,
    ).astype(jnp.float32)
    second_part, second_gain_grad, second_bias_grad = second_norm_back(normed_two_grad)
    second_grad = out_grad + second_part
    mixed_branch = lax.all_gather(second_grad.astype(jnp.bfloat16), "mp", axis=0, tiled=True)
    project_out_grad = contract_rows(mixed_flat, mixed_branch)
    mixed_grad = times_transposed(mixed_branch, project_out).astype(jnp.bfloat16)
    mixed_grad = mixed_grad.reshape(slices, length, heads_local, HEAD_DIM)
    packed_grad = lax.map(
        attend_slot_back, (queries, key_part, value_part, slot_valid, log_totals, mixed_grad)
    )
    packed_grad_low = packed_grad.reshape(tokens, heads_local * 3 * HEAD_DIM).astype(jnp.bfloat16)
    project_in_grad = contract_rows(normed_one_all, packed_grad_low)
    block_in = packed_grad_low
    normed_one_grad = lax.psum_scatter(
        times_transposed(block_in, project_in).astype(jnp.bfloat16),
        "mp",
        scatter_dimension=0,
        tiled=True,
    ).astype(jnp.float32)
    first_part, first_gain_grad, first_bias_grad = first_norm_back(normed_one_grad)
    first_grad = second_grad + first_part
    embed_branch = lax.all_gather(first_grad.astype(jnp.bfloat16), "mp", axis=0, tiled=True)
    embed_weight_grad = contract_rows(activated_low, embed_branch)
    activated_grad = times_transposed(embed_branch, embed_weight)
    stem_grad, group_gain_grad, group_bias_grad = stem_norm_back(activated_grad)
    stem_grad_low = stem_grad.astype(jnp.bfloat16)
    standard_grad = contract_rows(features, stem_grad_low)
    stem_weight_grad = standard_back(standard_grad)[0]
    features_grad = narrow_product(stem_grad_low, standard_use, True)
    up_weight_grad, up_bias_grad, down_weight_grad = sum_feed(
        up_weight_grad, up_bias_grad, down_weight_grad
    )
    (
        stem_weight_grad,
        group_gain_grad,
        group_bias_grad,
        embed_weight_grad,
        project_in_grad,
        project_out_grad,
    ) = lax.psum(
        (
            stem_weight_grad,
            group_gain_grad,
            group_bias_grad,
            embed_weight_grad,
            project_in_grad,
            project_out_grad,
        ),
        "dp",
    )
    first_gain_grad, first_bias_grad, second_gain_grad, second_bias_grad = lax.psum(
        (first_gain_grad, first_bias_grad, second_gain_grad, second_bias_grad), ("dp", "mp")
    )
    return (
        block_out,
        features_grad,
        stem_weight_grad,
        group_gain_grad,
        group_bias_grad,
        embed_weight_grad,
        first_gain_grad,
        first_bias_grad,
        project_in_grad,
        project_out_grad,
        second_gain_grad,
        second_bias_grad,
        up_weight_grad,
        up_bias_grad,
        down_weight_grad,
    )


def solution(mesh):
    return jax.shard_map(
        body,
        mesh=mesh,
        in_specs=(
            P("dp", None),
            P(None, "mp"),
            P("mp"),
            P("mp"),
            P("mp", None),
            P(),
            P(),
            P(None, "mp"),
            P("mp", None),
            P(),
            P(),
            P(None, "mp"),
            P("mp"),
            P("mp", None),
            P(),
            P("dp"),
            P(("dp", "mp"), None),
        ),
        out_specs=(
            P(("dp", "mp"), None),
            P(("dp", "mp"), None),
            P(None, "mp"),
            P("mp"),
            P("mp"),
            P("mp", None),
            P(),
            P(),
            P(None, "mp"),
            P("mp", None),
            P(),
            P(),
            P(None, "mp"),
            P("mp"),
            P("mp", None),
        ),
        check_vma=False,
    )
```

profile of v0, /device:TPU:0, one launch (start us, length us, event | category | flops | bytes accessed | tf_op | source)
XLA Modules:
  0.0 817.2 jit_solution(14272197429255868243)
XLA Ops:
  14.0 3.1 reshape.345
  21.2 2.7 copy.97
  25.0 2.7 copy.99
  27.7 5.5 multiply_convert_fusion.2
  33.2 2.5 fusion.123
  35.8 43.2 %reduce-scatter.7.cloned.1.call-done = f32[288,768]{1,0:T(8,128)} async-done(((f32[1152,768]{1,0:T(8,128)}), f32[288,768]{1,0:T(8,128)}) %reduce-scatter.7.cloned.1.call-update) | async-done | bytes 884752 | tf_op jit(solution)/shard_map/reduce_scatter | solution.py:61
  82.0 20.6 %all-gather.6.cloned.1.call-done = bf16[1152,768]{1,0:T(8,128)(2,1)} async-done(((bf16[288,768]{1,0:T(8,128)(2,1)}), bf16[1152,768]{1,0:T(8,128)(2,1)}) %all-gather.6.cloned.1.call-update) | async-done | bytes 1769488 | tf_op jit(solution)/shard_map/all_gather | solution.py:153
  102.6 4.1 convolution_convert_fusion.3
  106.7 4.5 reshape.346
  111.3 2.4 fusion.122
  115.7 11.4 %while.22 = (s32[]{:T(128)}, bf16[2,576,3,64]{1,3,2,0:T(8,128)(2,1)}, f32[2,3,576,1]{2,1,3,0:T(4,128)}, bf16[2,576,3,64]{1,3,2,0:T(8,128)(2,1)}, f32[2,576]{1,0:...) while((s32[]{:T(128)}, ...), condition=%wide.region_11.12_spmd, body=%wide.region_8.0_spmd.sunk | while | flops 265862016 | bytes 18747000 | solution.py:162
  131.6 3.5 fusion.124
  135.2 40.5 %reduce-scatter.9.cloned.1.call-done = f32[288,768]{1,0:T(8,128)} async-done(((f32[1152,768]{1,0:T(8,128)}), f32[288,768]{1,0:T(8,128)}) %reduce-scatter.9.cloned.1.call-update) | async-done | bytes 884752 | tf_op jit(solution)/shard_map/reduce_scatter | solution.py:61
  184.8 16.4 %all-gather.8.cloned.1.call-done = bf16[1152,768]{1,0:T(8,128)(2,1)} async-done(((bf16[288,768]{1,0:T(8,128)(2,1)}), bf16[1152,768]{1,0:T(8,128)(2,1)}) %all-gather.8.cloned.1.call-update) | async-done | bytes 1769488 | tf_op jit(solution)/shard_map/all_gather | solution.py:166
  201.2 5.1 convolution_add_fusion
  206.3 17.7 %all-gather.10.cloned.1.call-done = bf16[1152,768]{1,0:T(8,128)(2,1)} async-done(((bf16[288,768]{1,0:T(8,128)(2,1)}), bf16[1152,768]{1,0:T(8,128)(2,1)}) %all-gather.10.cloned.1.call-update) | async-done | bytes 1769488 | tf_op jit(solution)/shard_map/all_gather | solution.py:179
  224.0 12.8 %convert_reduce_fusion = (f32[768]{0:T(1024)}, bf16[1152,768]{1,0:T(8,128)(2,1)S(1)}, f32[1152,768]{1,0:T(8,128)}) fusion(f32[1152,768]{1,0:T(8,128)} %convolution_add_fusion, bf16[1152,768]{1,0:T(8,128)(2,1)} %all-gather.10.cloned.1.call-done, bf16[768,768]{1,0:T(8,128)(2,1)} %param.34), kind=kOutput, calls=%fused_computation.65 | convolution fusion | flops 1424424192 | bytes 11799552 | tf_op jit(solution)/shard_map/dot_general | solution.py:49
  238.1 2.8 convolution_convert_fusion.1
  241.0 3.6 multiply_convert_fusion.1
  245.8 2.8 convolution_convert_fusion.2
  248.7 21.8 %reduce-scatter.13.cloned.1.call-done = bf16[288,768]{1,0:T(8,128)(2,1)} async-done(((bf16[1152,768]{1,0:T(8,128)(2,1)}), bf16[288,768]{1,0:T(8,128)(2,1)}) %reduce-scatter.13.cloned.1.call-update) | async-done | bytes 442384 | tf_op jit(solution)/shard_map/reduce_scatter | solution.py:186
  274.0 29.2 %reduce-scatter.11.cloned.1.call-done = bf16[288,768]{1,0:T(8,128)(2,1)} async-done(((bf16[1152,768]{1,0:T(8,128)(2,1)}), bf16[288,768]{1,0:T(8,128)(2,1)}) %reduce-scatter.11.cloned.1.call-update) | async-done | bytes 442384 | tf_op jit(solution)/shard_map/reduce_scatter | solution.py:171
  303.2 2.7 fusion.117
  308.1 20.7 %all-gather.12.cloned.1.call-done = bf16[1152,768]{1,0:T(8,128)(2,1)} async-done(((bf16[288,768]{1,0:T(8,128)(2,1)}), bf16[1152,768]{1,0:T(8,128)(2,1)}) %all-gather.12.cloned.1.call-update) | async-done | bytes 1769488 | tf_op jit(solution)/shard_map/all_gather | solution.py:194
  328.7 3.0 convolution_convert_fusion.4
  335.9 21.0 %while.23 = (s32[]{:T(128)}, bf16[2,576,3,3,64]{1,4,2,3,0:T(8,128)(2,1)}, bf16[2,576,3,64]{1,3,2,0:T(8,128)(2,1)}, f32[2,576]{1,0:T(2,128)S(1)}, bf16[2,576,3,64...) while((s32[]{:T(128)}, ...), condition=%wide.region_21.22_spmd, body=%wide.region_19.21_spmd.sunk | while | flops 654371712 | bytes 52802980 | solution.py:198
  356.9 4.0 copy.107
  360.9 4.2 convert_element_type.119
  365.1 4.4 convolution_convert_fusion
  369.5 29.5 %reduce-scatter.15.cloned.1.call-done = bf16[288,768]{1,0:T(8,128)(2,1)} async-done(((bf16[1152,768]{1,0:T(8,128)(2,1)}), bf16[288,768]{1,0:T(8,128)(2,1)}) %reduce-scatter.15.cloned.1.call-update) | async-done | bytes 442384 | tf_op jit(solution)/shard_map/reduce_scatter | solution.py:204
  405.5 3.0 sub.100
  410.0 3.0 mul.487
  413.0 5.3 fusion.129
  418.4 3.2 fusion.128
  422.9 2.5 fusion.130
  425.5 3.2 fusion.125
  428.7 3.1 reshape.349
  431.8 6.0 multiply_reduce_fusion.1
  441.9 3.2 broadcast_in_dim.114
  446.6 3.0 broadcast_in_dim.116
  449.6 7.3 multiply_add_fusion.1
  461.9 4.1 fusion.109
  466.7 43.8 %all-reduce = (f32[768]{0:T(1024)}, f32[768]{0:T(1024)}, f32[768]{0:T(1024)}, f32[768]{0:T(1024)}) all-reduce(f32[768]{0:T(1024)S(1)} %get-tuple-element.190, f32[768]{0:T(1024)S(1)} %get-tuple-element.197, f32[768]{0:T(1024)S(1)} %copy-done.55, f32[768]{0:T(1024)S(1)} %copy-done.56), channel_id=1, replica_groups=mesh['dp'=8,'mp'=4] {'dp','mp'}, use_global_device_ids=true, to_apply=%region_37.38 | all-reduce | flops 3072 | bytes 24576 | tf_op jit(solution)/shard_map/psum | solution.py:241
  512.4 22.7 %all-reduce.1 = (f32[256]{0:T(256)}, f32[256]{0:T(256)}, f32[768]{0:T(1024)}) all-reduce(f32[256]{0:T(256)S(1)} %get-tuple-element.195, f32[256]{0:T(256)S(1)} %get-tuple-element.194, f32[768]{0:T(1024)S(1)} %copy-done.69), channel_id=1, replica_groups=mesh['dp'=8,'mp'=4] {'dp'}, use_global_device_ids=true, to_apply=%region_32.33 | all-reduce | flops 1280 | bytes 10240 | tf_op jit(solution)/shard_map/psum | solution.py:230
  535.1 216.7 %all-reduce.5.cloned.1.call-done = (f32[1024,256]{0,1:T(8,128)}, f32[256,768]{1,0:T(8,128)}, f32[768,576]{0,1:T(8,128)}, f32[192,768]{1,0:T(8,128)}, f32[768,768]{1,0:T(8,128)}, /*index=5*/f32[768,768]{1,0:T(8,128)}) async-done(((f32[1024,256]{0,1:T(8,128)}, f32[256,768]{1,0:T(8,128)}, f32[768,576]{0,1:T(8,128)}, f32[192,768]{1,0:T(8,128)}, f32[768,768]{1,0:T(8,128)}, /*index=5*/f32[768,768]{1,0:T(8,128)}), ...) | async-done | bytes 8912912 | tf_op jit(solution)/shard_map/psum | solution.py:230
  751.8 2.6 copy.117
  754.4 47.0 %reduce-scatter.17.cloned.1.call-done = f32[288,1024]{1,0:T(8,128)} async-done(((f32[1152,1024]{1,0:T(8,128)}), f32[288,1024]{1,0:T(8,128)}) %reduce-scatter.17.cloned.1.call-update) | async-done | bytes 1179664 | tf_op jit(solution)/shard_map/reduce_scatter | solution.py:61
  802.2 2.9 copy.174
  (301 shorter events, 103.1 us)
Async XLA Ops:
  7.2 4.8 copy-start
  7.2 71.8 %reduce-scatter.7.cloned.1.call-start = ((), (), s32[]{:S(2)}) async-start(), calls=%async_computation.6 | async-start | bytes 4423680 | tf_op jit(solution)/shard_map/reduce_scatter | solution.py:61
  10.3 8.9 %copy-start.65 = (f32[2]{0:T(128)}, f32[2]{0:T(128)S(1)}, u32[]{:S(2)}) copy-start(f32[2]{0:T(128)S(1)} %broadcast_multiply_fusion.3) | copy-start | bytes 28
  18.8 5.1 copy-start.41
  19.8 4.1 copy-start.46
  25.0 2.7 copy-start.63
  27.7 5.5 copy-start.25
  35.7 45.0 %copy-start.67 = (f32[768]{0:T(1024)S(1)}, f32[768]{0:T(1024)}, u32[]{:S(2)}) copy-start(f32[768]{0:T(1024)} %param.27) | copy-start | bytes 9220
  35.7 45.0 %copy-start.35 = (f32[768]{0:T(1024)S(1)}, f32[768]{0:T(1024)}, u32[]{:S(2)}) copy-start(f32[768]{0:T(1024)} %param.26) | copy-start | bytes 9220
  35.7 66.9 %all-gather.6.cloned.1.call-start = ((), (), s32[]{:S(2)}) async-start(), calls=%async_computation.7 | async-start | bytes 2211840 | tf_op jit(solution)/shard_map/all_gather | solution.py:153
  80.7 26.1 %copy-start.52 = (f32[288]{0:T(512)}, f32[288]{0:T(512)S(1)}, u32[]{:S(2)}) copy-start(f32[288]{0:T(512)S(1)} %multiply_reduce_fusion.6) | copy-start | bytes 3460
  80.7 26.0 %copy-start.43 = (f32[288]{0:T(512)}, f32[288]{0:T(512)S(1)}, u32[]{:S(2)}) copy-start(f32[288]{0:T(512)S(1)} %fusion.106) | copy-start | bytes 3460
  81.7 94.1 %reduce-scatter.9.cloned.1.call-start = ((), (), s32[]{:S(2)}) async-start(), calls=%async_computation.8 | async-start | bytes 4423680 | tf_op jit(solution)/shard_map/reduce_scatter | solution.py:61
  127.1 4.5 copy-start.34
  135.2 66.0 %all-gather.8.cloned.1.call-start = ((), (), s32[]{:S(2)}) async-start(), calls=%async_computation.9 | async-start | bytes 2211840 | tf_op jit(solution)/shard_map/all_gather | solution.py:166
  180.3 43.7 %all-gather.10.cloned.1.call-start = ((), (), s32[]{:S(2)}) async-start(), calls=%async_computation.11 | async-start | bytes 2211840 | tf_op jit(solution)/shard_map/all_gather | solution.py:179
  184.3 86.1 %reduce-scatter.13.cloned.1.call-start = ((), (), s32[]{:S(2)}) async-start(), calls=%async_computation.12 | async-start | bytes 2211840 | tf_op jit(solution)/shard_map/reduce_scatter | solution.py:186
  224.0 14.1 %copy-start.72 = (bf16[768,768]{1,0:T(8,128)(2,1)S(1)}, bf16[768,768]{1,0:T(8,128)(2,1)}, u32[]{:S(2)}) copy-start(bf16[768,768]{1,0:T(8,128)(2,1)} %param.32) | copy-start | bytes 3538948
  240.9 62.3 %reduce-scatter.11.cloned.1.call-start = ((), (), s32[]{:S(2)}) async-start(), calls=%async_computation.10 | async-start | bytes 2211840 | tf_op jit(solution)/shard_map/reduce_scatter | solution.py:171
  241.0 4.9 copy-start.73
  248.6 80.1 %all-gather.12.cloned.1.call-start = ((), (), s32[]{:S(2)}) async-start(), calls=%async_computation.13 | async-start | bytes 2211840 | tf_op jit(solution)/shard_map/all_gather | solution.py:194
  303.2 3.6 copy-start.17
  303.2 3.6 copy-start.37
  307.8 91.2 %reduce-scatter.15.cloned.1.call-start = ((), (), s32[]{:S(2)}) async-start(), calls=%async_computation.14 | async-start | bytes 2211840 | tf_op jit(solution)/shard_map/reduce_scatter | solution.py:204
  369.4 31.1 %copy-start.53 = (f32[288]{0:T(512)S(1)}, f32[288]{0:T(512)}, u32[]{:S(2)}) copy-start(f32[288]{0:T(512)} %copy-done.52) | copy-start | bytes 3460
  369.4 31.1 %copy-start.44 = (f32[288]{0:T(512)S(1)}, f32[288]{0:T(512)}, u32[]{:S(2)}) copy-start(f32[288]{0:T(512)} %copy-done.43) | copy-start | bytes 3460
  369.5 32.6 %copy-start.38 = (f32[288]{0:T(512)S(1)}, f32[288]{0:T(512)}, u32[]{:S(2)}) copy-start(f32[288]{0:T(512)} %copy-done.36) | copy-start | bytes 3460
  369.5 32.6 %copy-start.51 = (f32[288]{0:T(512)S(1)}, f32[288]{0:T(512)}, u32[]{:S(2)}) copy-start(f32[288]{0:T(512)} %copy-done.50) | copy-start | bytes 3460
  369.5 56.0 %all-gather.14.cloned.1.call-start = ((), (), s32[]{:S(2)}) async-start(), calls=%async_computation.15 | async-start | bytes 2211840 | tf_op jit(solution)/shard_map/all_gather | solution.py:212
  399.0 3.1 copy-start.10
  399.0 3.1 copy-start.18
  399.0 3.2 copy-start.20
  403.5 348.3 %all-reduce.5.cloned.1.call-start = ((), (), s32[]{:S(2)}) async-start(), calls=%async_computation.17 | async-start | bytes 17825792 | tf_op jit(solution)/shard_map/psum | solution.py:230
  413.0 5.3 copy-start.71
  413.0 5.3 copy-start.75
  418.3 3.2 copy-start.19
  418.3 3.2 copy-start.23
  418.4 4.6 copy-start.70
  431.8 6.0 copy-start.66
  431.8 6.0 copy-start.68
  446.6 3.0 copy-start.40
  449.6 7.3 copy-start.7
  449.6 7.3 copy-start.49
  461.9 339.5 %reduce-scatter.17.cloned.1.call-start = ((), (), s32[]{:S(2)}) async-start(), calls=%async_computation.16 | async-start | bytes 5898240 | tf_op jit(solution)/shard_map/reduce_scatter | solution.py:61
  466.0 46.3 %copy-start.69 = (f32[768]{0:T(1024)S(1)}, f32[768]{0:T(1024)}, u32[]{:S(2)}) copy-start(f32[768]{0:T(1024)} %get-tuple-element.244) | copy-start | bytes 9220
  751.8 49.6 %copy-start.30 = (f32[256,768]{1,0:T(8,128)S(1)}, f32[256,768]{1,0:T(8,128)}, u32[]{:S(2)}) copy-start(f32[256,768]{1,0:T(8,128)} %get-tuple-element.434) | copy-start | bytes 2359300
  802.2 3.0 copy-start.31
  802.2 3.8 copy-start.22
  (49 other events, 70.4 us)
Sparse Core Ops, SparseCore 0:
  35.8 43.1 reduce-scatter.6
  81.8 20.7 all-gather.5
  135.3 40.4 reduce-scatter.8
  180.4 20.7 all-gather.7
  203.2 20.7 all-gather.9
  241.0 29.3 reduce-scatter.12
  273.8 29.3 reduce-scatter.10
  307.9 20.7 all-gather.11
  369.6 29.3 reduce-scatter.14
  403.6 20.7 all-gather.13
  462.0 289.7 all-reduce.4
  754.7 46.5 reduce-scatter.16
where the time goes:
time: 824 us; the launch traced here: 817 us
  waiting for transfers between devices  503 us (61%)
  local copies, waits for them, and re-layouts  88 us (11%)
  matrix products  83.4 us (10%)
  blocking collectives  66.5 us (8%)
  other arithmetic  58.9 us (7%)
  between operations  15.2 us (2%)
    psum x1, waiting for transfers between devices, body(): lax.psum((stem_weight_grad, group_gain_grad, group_bias_grad, embed_weigh...  217 us
    reduce_scatter x3, waiting for transfers between devices, narrow_product(): lax.psum_scatter(plain_or_transposed(block_in, weight, transposed), 'mp',...  131 us
    psum x1, blocking collectives, body(): lax.psum((first_gain_grad, first_bias_grad, second_gain_grad, second_bias...  43.8 us
    dot_general x6, matrix products, times_transposed(): lax.dot_general(left, right, (((1,), (1,)), ((), ())), preferred_element_...  30.2 us
    reduce_scatter x1, waiting for transfers between devices, body(): lax.psum_scatter(times_transposed(block_in, project_in).astype(jnp.bfloat...  29.5 us
    reduce_scatter x1, waiting for transfers between devices, body(): lax.psum_scatter(jnp.dot(block_in, down_weight, preferred_element_type=jn...  29.2 us
    psum x1, blocking collectives, body(): lax.psum((stem_weight_grad, group_gain_grad, group_bias_grad, embed_weigh...  22.7 us
    reduce_scatter x1, waiting for transfers between devices, body(): lax.psum_scatter(times_transposed(block_in, up_weight).astype(jnp.bfloat1...  21.8 us
  transfers between devices with their start and end apart: 12, of which 11 were waited for; matrix products, arithmetic and copies ran while one was open for 6% of the time, Pallas kernels for 0%

commit v1 on v0

v1 whole, which is shorter than its diff:
```python
import functools

import jax
import jax.numpy as jnp
from jax import lax
from jax.experimental import pallas as pl
from jax.experimental.pallas import tpu as pltpu
from jax.sharding import PartitionSpec as P

MESH = pl.DeviceIdType.MESH
F32 = jnp.float32
BF16 = jnp.bfloat16
HEAD_DIM = 64
GROUP = 32
NEAR = 8


def dot(left, right, left_dim=1, right_dim=0, precision=None):
    return lax.dot_general(
        left,
        right,
        (((left_dim,), (right_dim,)), ((), ())),
        precision=precision,
        preferred_element_type=F32,
    )


def gelu_parts(z):
    cdf = 0.5 + 0.5 * lax.erf(z * 0.7071067811865476)
    return z * cdf, cdf + z * (jnp.exp(-0.5 * z * z) * 0.3989422804014327)


class Net:
    def __init__(self, send_sems, recv_sems, local_sems):
        self.send_sems, self.recv_sems, self.local_sems = send_sems, recv_sems, local_sems
        self.count, self.local_count, self.unsent = 0, 0, []

    def send(self, src, dst, device):
        copy = pltpu.make_async_remote_copy(
            src_ref=src,
            dst_ref=dst,
            send_sem=self.send_sems.at[self.count],
            recv_sem=self.recv_sems.at[self.count],
            device_id=device,
            device_id_type=MESH,
        )
        self.count += 1
        copy.start()
        self.unsent.append(copy)
        return copy

    def sent(self, copy):
        self.unsent = [one for one in self.unsent if one is not copy]
        copy.wait_send()

    def local(self, src, dst):
        copy = pltpu.make_async_copy(src, dst, self.local_sems.at[self.local_count])
        self.local_count += 1
        copy.start()
        return copy

    def finish(self):
        for copy in self.unsent:
            copy.wait_send()


class Summed:
    def __init__(self, net, place, grad, half_in, parts_in, piece, out):
        self.net, self.place = net, place
        self.grad, self.half_in, self.parts_in, self.piece, self.out = (
            grad,
            half_in,
            parts_in,
            piece,
            out,
        )
        self.rows = grad.shape[-2]
        self.part = self.rows // 4

    def start(self):
        y = self.place.y
        self.half = self.net.send(self.grad.at[1 - y], self.half_in, self.place.y_device)

    def spread(self):
        y, zi = self.place.y, self.place.zi
        self.half.wait_recv()
        for t in range(4):
            rows = pl.ds(t * self.part, self.part)
            self.grad[y, rows, :] = (
                self.grad[y, rows, :].astype(F32) + self.half_in[rows, :].astype(F32)
            ).astype(BF16)
        self.parts = []
        for k in range(1, 4):
            to = lax.rem(zi + k, 4)
            rows = pl.ds(pl.multiple_of(to * self.part, 16), self.part)
            self.parts.append(
                self.net.send(
                    self.grad.at[y, rows], self.parts_in.at[k - 1], self.place.z_device(k)
                )
            )

    def gather(self):
        y, zi = self.place.y, self.place.zi
        rows = pl.ds(pl.multiple_of(zi * self.part, 16), self.part)
        for copy in self.parts:
            copy.wait_recv()
        total = self.grad[y, rows, :].astype(F32)
        for k in range(3):
            total = total + self.parts_in[k].astype(F32)
        self.piece[...] = total.astype(BF16)
        target = self.out.at[y, rows]
        self.own = self.net.local(self.piece, target)
        self.pieces = [
            self.net.send(self.piece, target, self.place.z_device(k)) for k in range(1, 4)
        ]

    def share(self):
        y = self.place.y
        self.own.wait()
        for copy in self.pieces:
            copy.wait_recv()
        self.last = self.net.send(self.out.at[y], self.out.at[y], self.place.y_device)

    def done(self):
        self.last.wait_recv()


class Place:
    def __init__(self):
        self.d = lax.axis_index("dp")
        self.m = lax.axis_index("mp")
        self.x = lax.div(self.m, 2)
        self.c = lax.rem(self.m, 2)
        self.y = lax.rem(self.d, 2)
        self.zi = lax.div(lax.rem(self.d, NEAR), 2)
        self.base = self.d - lax.rem(self.d, NEAR)
        self.sib_m = self.m + 1 - 2 * self.c
        self.far_m = lax.rem(self.m + 2, 4)
        self.far_sib_m = lax.rem(self.sib_m + 2, 4)
        self.sib = (self.d, self.sib_m)
        self.far = (self.d, self.far_m)
        self.y_device = (self.d + 1 - 2 * self.y, self.m)

    def z_device(self, k):
        return (self.base + 2 * lax.rem(self.zi + k, 4) + self.y, self.m)


def kernel(in_names, out_names, scratch_names, *refs):
    names = in_names + out_names + scratch_names
    r = dict(zip(names, refs))
    run(**r)


def run(
    features, stem_weight, group_gain, group_bias, embed_weight, first_gain, first_bias,
    project_in, project_out, second_gain, second_bias, up_weight, up_bias, down_weight,
    valid_mask, slot_slice, cotangent,
    block_out, features_grad, o_stem, o_embed, o_pin, o_pout, o_up, o_down, o_small,
    feat, stem, std, wstat, embed, pin, pout, up, down, gvec, xhs, dgs, act, gst,
    sbuf, rbuf, res1, xh1, rs1, n1, q, k, v, probs, heads, mixed, res2, xh2, rs2,
    n2, hid, branch, preg, own, csend, crecv, xsend, xrecv, mb, pg, sg, gtmp,
    g_up, g_down, g_pin, g_pout, g_embed, g_stem,
    x_pin, x_pout, x_embed, x_stem,
    y_up, y_down, y_pin, y_pout, y_embed, y_stem,
    z_up, z_down, z_pin, z_pout, z_embed, z_stem,
    p_up, p_down, p_pin, p_pout, p_embed, p_stem,
    sm, smr, smz, send_sems, recv_sems, local_sems,
):
    place = Place()
    net = Net(send_sems, recv_sems, local_sems)
    x, c = place.x, place.c
    R = cotangent.shape[0]
    L = feat.shape[0]
    D = up.shape[0]
    own_rows = pl.multiple_of(c * R, 16)
    sib_rows = pl.multiple_of((1 - c) * R, 16)

    def block(m):
        return pl.ds(pl.multiple_of(m * R, 16), R)

    barrier = pltpu.get_barrier_semaphore()
    peers = [place.sib, place.far, place.y_device] + [place.z_device(i) for i in (1, 2, 3)]
    for peer in peers:
        pl.semaphore_signal(barrier, inc=1, device_id=peer, device_id_type=MESH)
    l_stem = net.local(stem_weight, stem.at[0])
    l_feat = net.local(features.at[pl.ds(pl.multiple_of(x * L, 16), L)], feat)
    l_embed = net.local(embed_weight, embed.at[0])
    l_cot = net.local(cotangent, branch.at[block(place.m)])
    l_pin = net.local(project_in, pin.at[0])
    l_pout = net.local(project_out, pout.at[0])
    l_up = net.local(up_weight, up)
    l_down = net.local(down_weight, down)
    gvec[0, 0:1, :] = group_gain[...].reshape(1, -1)
    gvec[0, 1:2, :] = group_bias[...].reshape(1, -1)
    pl.semaphore_wait(barrier, len(peers))

    c_gvec = net.send(gvec.at[0], gvec.at[1], place.far)
    c_stem = net.send(stem_weight, stem.at[1], place.far)

    slices = valid_mask.shape[0]
    lengths = jnp.sum(valid_mask[...].astype(F32), axis=1, keepdims=True)
    mine = lax.broadcasted_iota(jnp.int32, (slices, 1), 0) == slot_slice[x]
    length = jnp.sum(jnp.where(mine, lengths, 0.0), axis=0, keepdims=True)

    def valid_rows(start, count):
        at = (lax.broadcasted_iota(jnp.int32, (count, 1), 0) + start).astype(F32)
        return jnp.where(at < length, 1.0, 0.0)

    key_valid = jnp.where(
        lax.broadcasted_iota(jnp.int32, (1, L), 1).astype(F32) < length, 1.0, 0.0
    )
    score_scale = HEAD_DIM ** (-0.5)
    key_scale = key_valid * score_scale
    key_shift = (key_valid - 1.0) * 1e9

    channels = stem.shape[2]
    same = (
        lax.div(lax.broadcasted_iota(jnp.int32, (channels, channels), 0), GROUP)
        == lax.div(lax.broadcasted_iota(jnp.int32, (channels, channels), 1), GROUP)
    )
    same = jnp.where(same, 1.0, 0.0)

    def group_sum(values):
        wide = jnp.broadcast_to(values, (8, channels))
        return dot(wide, same, precision=lax.Precision.HIGHEST)[0:1]

    def standardize(j):
        w = stem[j].astype(F32)
        average = jnp.sum(w, axis=0, keepdims=True) * (1.0 / w.shape[0])
        w = w - average
        scale = lax.rsqrt(jnp.sum(w * w, axis=0, keepdims=True) * (1.0 / w.shape[0]) + 1e-5)
        std[j] = (w * scale).astype(BF16)
        wstat[j, 0:1, :] = average
        wstat[j, 1:2, :] = scale

    tile_rows = [(t * R, R) for t in range(L // R)]

    def stem_forward(j):
        count = 1.0 / (length * GROUP)
        total = jnp.zeros((1, channels), F32)
        for at, size in tile_rows:
            s = dot(feat[at : at + size, :], std[j])
            xhs[j, at : at + size, :] = s
            total = total + jnp.sum(s * valid_rows(at, size), axis=0, keepdims=True)
        average = group_sum(total) * count
        total = jnp.zeros((1, channels), F32)
        for at, size in tile_rows:
            s = xhs[j, at : at + size, :] - average
            total = total + jnp.sum(s * s * valid_rows(at, size), axis=0, keepdims=True)
        scale = lax.rsqrt(group_sum(total) * count + 1e-5)
        gst[j, 0:1, :] = scale
        for at, size in tile_rows:
            xh = (xhs[j, at : at + size, :] - average) * scale
            xhs[j, at : at + size, :] = xh
            value, slope = gelu_parts(xh * gvec[j, 0:1, :] + gvec[j, 1:2, :])
            act[j, at : at + size, :] = value.astype(BF16)
            dgs[j, at : at + size, :] = slope

    l_stem.wait()
    standardize(0)
    l_feat.wait()
    stem_forward(0)
    c_embed = net.send(embed_weight, embed.at[1], place.far)
    c_gvec.wait_recv()
    c_stem.wait_recv()
    standardize(1)
    c_pin = net.send(project_in, pin.at[1], place.far)
    stem_forward(1)
    l_embed.wait()
    c_embed.wait_recv()
    c_pout = net.send(project_out, pout.at[1], place.far)

    def core_sum(product):
        width = pl.ds(0, D)
        sbuf[:, width] = product(sib_rows)
        copy = net.send(sbuf.at[:, width], rbuf.at[:, width], place.sib)
        mine = product(own_rows)
        copy.wait_recv()
        net.sent(copy)
        return mine

    def embed_product(start):
        rows = pl.ds(start, R)
        return dot(act[0, rows, :], embed[0]) + dot(act[1, rows, :], embed[1])

    res1[...] = core_sum(embed_product)

    step = R // 3

    def layer_norm(res, other, add, gain, bias, xh_ref, scale_ref, out_ref, out_start):
        gain, bias = gain[...].reshape(1, -1), bias[...].reshape(1, -1)
        for t in range(3):
            rows = slice(t * step, (t + 1) * step)
            value = res[rows, :] + other[rows, 0:D]
            if add is not None:
                value = value + add[rows, :]
            res[rows, :] = value
            average = jnp.sum(value, axis=1, keepdims=True) * (1.0 / D)
            value = value - average
            scale = lax.rsqrt(jnp.sum(value * value, axis=1, keepdims=True) * (1.0 / D) + 1e-6)
            xh = value * scale
            xh_ref[rows, :] = xh
            scale_ref[rows, :] = scale
            out_ref[pl.ds(out_start + t * step, step), :] = (xh * gain + bias).astype(BF16)

    layer_norm(res1, rbuf, None, first_gain, first_bias, xh1, rs1, n1, own_rows)
    c_n1 = net.send(n1.at[pl.ds(own_rows, R)], n1.at[pl.ds(own_rows, R)], place.sib)
    l_pin.wait()
    c_n1.wait_recv()

    per_shard = pin.shape[2] // (3 * HEAD_DIM)

    def attend(j):
        for at, size in tile_rows:
            packed = dot(n1[at : at + size, :], pin[j]).astype(BF16)
            for h in range(per_shard):
                for i, ref in enumerate((q, k, v)):
                    lane = (3 * h + i) * HEAD_DIM
                    ref[per_shard * j + h, at : at + size, :] = packed[:, lane : lane + HEAD_DIM]

        def head(i, carry):
            h = per_shard * j + i
            for at, size in tile_rows:
                s = dot(q[h, at : at + size, :], k[h], 1, 1) * key_scale + key_shift
                s = jnp.exp(s - jnp.max(s, axis=1, keepdims=True))
                p = (s * (1.0 / jnp.sum(s, axis=1, keepdims=True))).astype(BF16)
                probs[h, at : at + size, :] = p
                heads[h, at : at + size, :] = dot(p, v[h]).astype(BF16)
            return carry

        lax.fori_loop(0, per_shard, head, 0)

    attend(0)
    c_pin.wait_recv()
    c_cot = [
        net.send(cotangent, branch.at[block(place.m)], device) for device in (place.far, place.sib)
    ]
    attend(1)

    def side_by_side(pieces, store):
        at = 0
        while at < len(pieces):
            pair = pieces[at : at + 2]
            value = pair[0] if len(pair) == 1 else jnp.concatenate(pair, axis=1)
            store(slice(at * HEAD_DIM, at * HEAD_DIM + value.shape[1]), value)
            at += 2

    def store_mixed(lanes, value):
        mixed[:, lanes] = value

    side_by_side([heads[h] for h in range(2 * per_shard)], store_mixed)
    l_pout.wait()
    c_pout.wait_recv()
    out_width = pout.shape[1]

    def out_product(start):
        rows = pl.ds(start, R)
        whole = jnp.concatenate([pout[0], pout[1]], axis=0)
        return dot(mixed[rows, :], whole)

    res2[...] = core_sum(out_product)
    layer_norm(
        res2, rbuf, res1, second_gain, second_bias, xh2, rs2, n2, pl.multiple_of(place.m * R, 16)
    )
    mine = block(place.m)
    c_n2 = [net.send(n2.at[mine], n2.at[mine], device) for device in (place.far, place.sib)]

    l_cot.wait()
    l_up.wait()
    l_down.wait()
    bias_sum = []

    def feed(m):
        rows = block(m)
        pre = dot(n2[rows, :], up[...]) + up_bias[...].reshape(1, -1)
        value, slope = gelu_parts(pre)
        hid[rows, :] = value.astype(BF16)
        grad = (dot(branch[rows, :], down[...], 1, 1) * slope).astype(BF16)
        preg[rows, :] = grad
        bias_sum.append(jnp.sum(grad.astype(F32), axis=0, keepdims=True))

    def back_part(m):
        return dot(preg[block(m), :], up[...], 1, 1)

    def out_part(m):
        return dot(hid[block(m), :], down[...])

    def mask_branch(m, own_slot):
        rows = block(m)
        start = lax.rem(m, 2) * R
        branch[rows, :] = (
            branch[rows, :].astype(F32) * valid_of(own_slot, start)
        ).astype(BF16)

    mine_far = lax.broadcasted_iota(jnp.int32, (slices, 1), 0) == slot_slice[1 - x]
    far_length = jnp.sum(jnp.where(mine_far, lengths, 0.0), axis=0, keepdims=True)

    def valid_of(own_slot, start):
        at = (lax.broadcasted_iota(jnp.int32, (R, 1), 0) + start).astype(F32)
        return jnp.where(at < (length if own_slot else far_length), 1.0, 0.0)

    c_cot[0].wait_recv()
    f_rows = block(place.far_m)
    c_cot_fwd = net.send(branch.at[f_rows], branch.at[f_rows], place.sib)
    mask_done = []

    mask_branch(place.m, True)
    feed(place.m)
    own[1] = back_part(place.m)
    c_cot[1].wait_recv()
    c_n2[1].wait_recv()
    mask_branch(place.sib_m, True)
    feed(place.sib_m)
    csend[1, 0] = back_part(place.sib_m).astype(BF16)
    c_core = {}
    c_core[1, 0] = net.send(csend.at[1, 0], crecv.at[1, 0], place.sib)
    c_n2[0].wait_recv()
    c_n2_fwd = net.send(n2.at[f_rows], n2.at[f_rows], place.sib)
    csend[0, 0] = out_part(place.sib_m).astype(BF16)
    c_core[0, 0] = net.send(csend.at[0, 0], crecv.at[0, 0], place.sib)
    own[0] = out_part(place.m)
    c_cot_fwd.wait_recv()
    c_n2_fwd.wait_recv()
    mask_branch(place.far_sib_m, False)
    feed(place.far_sib_m)
    csend[1, 1] = back_part(place.far_sib_m).astype(BF16)
    c_core[1, 1] = net.send(csend.at[1, 1], crecv.at[1, 1], place.sib)
    net.sent(c_cot_fwd)
    mask_branch(place.far_m, False)
    feed(place.far_m)
    sbuf[:, 0:D] = back_part(place.far_m)
    c_core[1, 1].wait_recv()
    xsend[1] = (sbuf[:, 0:D] + crecv[1, 1].astype(F32)).astype(BF16)
    c_far = {}
    c_far[1] = net.send(xsend.at[1], xrecv.at[1], place.far)
    csend[0, 1] = out_part(place.far_sib_m).astype(BF16)
    c_core[0, 1] = net.send(csend.at[0, 1], crecv.at[0, 1], place.sib)
    sbuf[:, 0:D] = out_part(place.far_m)
    c_core[0, 1].wait_recv()
    xsend[0] = (sbuf[:, 0:D] + crecv[0, 1].astype(F32)).astype(BF16)
    c_far[0] = net.send(xsend.at[0], xrecv.at[0], place.far)

    summed = {
        "down": Summed(net, place, g_down, y_down, z_down, p_down, o_down),
        "up": Summed(net, place, g_up, y_up, z_up, p_up, o_up),
        "pout": Summed(net, place, g_pout.at[0], y_pout, z_pout, p_pout, o_pout),
        "pin": Summed(net, place, g_pin.at[0], y_pin, z_pin, p_pin, o_pin),
        "embed": Summed(net, place, g_embed.at[0], y_embed, z_embed, p_embed, o_embed),
        "stem": Summed(net, place, g_stem.at[0], y_stem, z_stem, p_stem, o_stem),
    }

    half = D // 2
    for i in range(2):
        g_down[i] = dot(hid[:, i * half : (i + 1) * half], branch[...], 0, 0).astype(BF16)
    summed["down"].start()
    for i in range(2):
        g_up[i] = dot(n2[:, i * half : (i + 1) * half], preg[...], 0, 0).astype(BF16)
    summed["up"].start()
    sm[...] = jnp.zeros_like(sm)
    sm[4:5, :] = bias_sum[0] + bias_sum[1] + bias_sum[2] + bias_sum[3]

    def norm_back(grad_of, gain, xh_ref, scale_ref, keep, out_ref, out_start, row):
        gain = gain[...].reshape(1, -1)
        gain_sum = jnp.zeros((1, D), F32)
        bias_total = jnp.zeros((1, D), F32)
        for t in range(3):
            rows = slice(t * step, (t + 1) * step)
            dy, through = grad_of(rows)
            xh = xh_ref[rows, :]
            gain_sum = gain_sum + jnp.sum(dy * xh, axis=0, keepdims=True)
            bias_total = bias_total + jnp.sum(dy, axis=0, keepdims=True)
            dy = dy * gain
            mean_one = jnp.sum(dy, axis=1, keepdims=True) * (1.0 / D)
            mean_two = jnp.sum(dy * xh, axis=1, keepdims=True) * (1.0 / D)
            dx = through + scale_ref[rows, :] * (dy - mean_one - xh * mean_two)
            if keep is not None:
                keep[rows, :] = dx
            out_ref[pl.ds(out_start + t * step, step), :] = dx.astype(BF16)
        sm[row : row + 1, :] = gain_sum
        sm[row + 1 : row + 2, :] = bias_total

    sg2, eb = res1, mb
    c_core[1, 0].wait_recv()
    c_far[1].wait_recv()

    def second_grad_of(rows):
        dy = own[1, rows, :] + crecv[1, 0, rows, :].astype(F32) + xrecv[1, rows, :].astype(F32)
        at = pl.ds(pl.multiple_of(place.m * R, 16) + rows.start, step)
        return dy, branch[at, :].astype(F32)

    norm_back(second_grad_of, second_gain, xh2, rs2, sg2, mb, own_rows, 2)
    c_mb = net.send(mb.at[pl.ds(own_rows, R)], mb.at[pl.ds(own_rows, R)], place.sib)

    c_core[0, 0].wait_recv()
    c_far[0].wait_recv()
    net.sent(c_core[0, 0])
    for t in range(3):
        rows = slice(t * step, (t + 1) * step)
        value = (
            res2[rows, :]
            + own[0, rows, :]
            + crecv[0, 0, rows, :].astype(F32)
            + xrecv[0, rows, :].astype(F32)
        )
        csend[0, 0, rows, :] = (value * valid_rows(own_rows + t * step, step)).astype(BF16)
    l_bout = net.local(csend.at[0, 0], block_out)

    c_mb.wait_recv()
    grad = dot(mixed[...], mb[...], 0, 0)
    shard = pout.shape[1]
    wide = g_pout.shape[3]
    for j in (1, 0):
        for i in range(2):
            g_pout[j, i] = grad[j * shard : (j + 1) * shard, i * wide : (i + 1) * wide].astype(BF16)
    cx = {}
    cx["pout"] = net.send(g_pout.at[1], x_pout, place.far)
    whole_out = jnp.concatenate([pout[0], pout[1]], axis=0)
    for at, size in tile_rows:
        value = dot(mb[at : at + size, :], whole_out, 1, 1).astype(BF16)
        for h in range(2 * per_shard):
            heads[h, at : at + size, :] = value[:, h * HEAD_DIM : (h + 1) * HEAD_DIM]

    def head_back(h, carry):
        p = probs[h]
        dp = dot(heads[h], v[h], 1, 1)
        v[h] = dot(p, heads[h], 0, 0).astype(BF16)
        p = p.astype(F32)
        ds = (p * (dp - jnp.sum(p * dp, axis=1, keepdims=True))).astype(BF16)
        dq = (dot(ds, k[h]) * score_scale).astype(BF16)
        k[h] = (dot(ds, q[h], 0, 0) * score_scale).astype(BF16)
        q[h] = dq
        return carry

    lax.fori_loop(0, 2 * per_shard, head_back, 0)

    for j in (1, 0):

        def store_pg(lanes, value):
            pg[j, :, lanes] = value

        pieces = [ref[per_shard * j + h] for h in range(per_shard) for ref in (q, k, v)]
        side_by_side(pieces, store_pg)
    for j in (1, 0):
        for i in range(2):
            g_pin[j, i] = dot(n1[:, i * half : (i + 1) * half], pg[j], 0, 0).astype(BF16)
        if j == 1:
            cx["pin"] = net.send(g_pin.at[1], x_pin, place.far)

    def first_product(start):
        rows = pl.ds(start, R)
        return dot(pg[0, rows, :], pin[0], 1, 1) + dot(pg[1, rows, :], pin[1], 1, 1)

    own[0] = core_sum(first_product)

    def first_grad_of(rows):
        return own[0, rows, :] + rbuf[rows, 0:D], sg2[rows, :]

    net.sent(c_mb)
    norm_back(first_grad_of, first_gain, xh1, rs1, None, eb, own_rows, 0)
    c_eb = net.send(eb.at[pl.ds(own_rows, R)], eb.at[pl.ds(own_rows, R)], place.sib)

    def far_sum(name, grad, arrived):
        cx[name].wait_recv()
        for i in range(2):
            grad[0, i] = (grad[0, i].astype(F32) + arrived[i].astype(F32)).astype(BF16)
        summed[name].start()

    summed["down"].spread()
    far_sum("pout", g_pout, x_pout)
    c_eb.wait_recv()

    embed_half = embed.shape[1] // 2
    for j in (1, 0):
        grad = dot(act[j], eb[...], 0, 0)
        for i in range(2):
            g_embed[j, i] = grad[i * embed_half : (i + 1) * embed_half, :].astype(BF16)
        if j == 1:
            cx["embed"] = net.send(g_embed.at[1], x_embed, place.far)
    cin = feat.shape[1]
    for j in (1, 0):
        gain_sum = jnp.zeros((1, channels), F32)
        bias_total = jnp.zeros((1, channels), F32)
        for at, size in tile_rows:
            dz = dot(eb[at : at + size, :], embed[j], 1, 1) * dgs[j, at : at + size, :]
            dgs[j, at : at + size, :] = dz
            gain_sum = gain_sum + jnp.sum(dz * xhs[j, at : at + size, :], axis=0, keepdims=True)
            bias_total = bias_total + jnp.sum(dz, axis=0, keepdims=True)
        sm[5 + j : 6 + j, 0:channels] = gain_sum
        sm[5 + j : 6 + j, channels : 2 * channels] = bias_total
        gain = gvec[j, 0:1, :]
        count = 1.0 / (length * GROUP)
        mean_one = group_sum(bias_total * gain) * count
        mean_two = group_sum(gain_sum * gain) * count
        for at, size in tile_rows:
            part = dgs[j, at : at + size, :] * gain - valid_rows(at, size) * (
                mean_one + xhs[j, at : at + size, :] * mean_two
            )
            sg[j, at : at + size, :] = (part * gst[j, 0:1, :]).astype(BF16)
        average, scale = wstat[j, 0:1, :], wstat[j, 1:2, :]
        sum_one = jnp.zeros((1, channels), F32)
        sum_two = jnp.zeros((1, channels), F32)
        quarter = cin // 4
        for t in range(4):
            rows = slice(t * quarter, (t + 1) * quarter)
            grad = dot(feat[:, rows], sg[j], 0, 0)
            gtmp[rows, :] = grad
            xh = (stem[j, rows, :].astype(F32) - average) * scale
            sum_one = sum_one + jnp.sum(grad, axis=0, keepdims=True)
            sum_two = sum_two + jnp.sum(grad * xh, axis=0, keepdims=True)
        sum_one = sum_one * (1.0 / cin)
        sum_two = sum_two * (1.0 / cin)
        for t in range(4):
            rows = slice(t * quarter, (t + 1) * quarter)
            xh = (stem[j, rows, :].astype(F32) - average) * scale
            value = (gtmp[rows, :] - sum_one - xh * sum_two) * scale
            g_stem[j, t // 2, (t % 2) * quarter : (t % 2 + 1) * quarter, :] = value.astype(BF16)
        if j == 1:
            cx["stem"] = net.send(g_stem.at[1], x_stem, place.far)

    c_sm = net.send(sm, smr.at[0], place.sib)
    summed["up"].spread()
    summed["down"].gather()
    far_sum("pin", g_pin, x_pin)
    c_sm.wait_recv()
    net.sent(c_sm)
    sm[0:4, :] = sm[0:4, :] + smr[0, 0:4, :]
    c_sm = net.send(sm, smr.at[1], place.far)

    def feature_product(start):
        rows = pl.ds(start, R)
        return dot(sg[0, rows, :], std[0], 1, 1) + dot(sg[1, rows, :], std[1], 1, 1)

    sbuf[...] = feature_product(sib_rows)
    c_feat = net.send(sbuf, rbuf, place.sib)
    mine_feat = feature_product(own_rows)
    c_feat.wait_recv()
    net.sent(c_feat)
    sbuf[...] = mine_feat + rbuf[...]
    l_fgrad = net.local(sbuf, features_grad)

    far_sum("embed", g_embed, x_embed)
    c_sm.wait_recv()
    net.sent(c_sm)
    sm[0:4, :] = sm[0:4, :] + smr[1, 0:4, :]
    sm[5:6, :] = sm[5:6, :] + smr[1, 6:7, :]
    c_sm = net.send(sm, smr.at[2], place.y_device)
    summed["pout"].spread()
    summed["up"].gather()
    far_sum("stem", g_stem, x_stem)
    summed["down"].share()
    c_sm.wait_recv()
    net.sent(c_sm)
    smz[place.zi] = sm[...] + smr[2]
    c_smz = [
        net.send(smz.at[place.zi], smz.at[place.zi], place.z_device(i)) for i in (1, 2, 3)
    ]
    summed["pout"].gather()
    summed["pin"].spread()
    summed["up"].share()
    summed["embed"].spread()
    summed["pin"].gather()
    summed["pout"].share()
    summed["stem"].spread()
    for copy in c_smz:
        copy.wait_recv()
    o_small[...] = smz[0] + smz[1] + smz[2] + smz[3]
    summed["embed"].gather()
    summed["pin"].share()
    summed["stem"].gather()
    summed["embed"].share()
    summed["stem"].share()
    l_bout.wait()
    l_fgrad.wait()
    for one in summed.values():
        one.done()
    net.finish()


def body(
    features, stem_weight, group_gain, group_bias, embed_weight, first_gain, first_bias,
    project_in, project_out, second_gain, second_bias, up_weight, up_bias, down_weight,
    valid_mask, slot_slice, cotangent, *, dp,
):
    slots = slot_slice.shape[0]
    L = features.shape[0] // slots
    R = cotangent.shape[0]
    cin, channels = stem_weight.shape
    D = cotangent.shape[1]
    wide_in = project_in.shape[1]
    out_rows = project_out.shape[0]
    hidden = up_weight.shape[1]
    heads = 2 * wide_in // (3 * HEAD_DIM)
    hbm = pl.BlockSpec(memory_space=pl.ANY)
    vmem = pl.BlockSpec(memory_space=pltpu.VMEM)
    smem = pl.BlockSpec(memory_space=pltpu.SMEM)
    in_specs = dict(
        features=hbm, stem_weight=hbm, group_gain=vmem, group_bias=vmem, embed_weight=hbm,
        first_gain=vmem, first_bias=vmem, project_in=hbm, project_out=hbm, second_gain=vmem,
        second_bias=vmem, up_weight=hbm, up_bias=vmem, down_weight=hbm, valid_mask=vmem,
        slot_slice=smem, cotangent=hbm,
    )
    grads = dict(
        up=(D // 2, hidden),
        down=(hidden // 2, D),
        pin=(D // 2, wide_in),
        pout=(out_rows, D // 2),
        embed=(channels // 2, D),
        stem=(cin // 2, channels),
    )
    outs = dict(block_out=((R, D), BF16, hbm), features_grad=((R, cin), F32, hbm))
    for name in ("stem", "embed", "pin", "pout", "up", "down"):
        outs["o_" + name] = ((2,) + grads[name], BF16, hbm)
    outs["o_small"] = ((8, D), F32, vmem)
    scratch = dict(
        feat=((L, cin), BF16), stem=((2, cin, channels), BF16), std=((2, cin, channels), BF16),
        wstat=((2, 8, channels), F32), embed=((2, channels, D), BF16), pin=((2, D, wide_in), BF16),
        pout=((2, out_rows, D), BF16), up=((D, hidden), BF16), down=((hidden, D), BF16),
        gvec=((2, 8, channels), F32), xhs=((2, L, channels), F32), dgs=((2, L, channels), F32),
        act=((2, L, channels), BF16), gst=((2, 8, channels), F32),
        sbuf=((R, cin), F32), rbuf=((R, cin), F32), res1=((R, D), F32), xh1=((R, D), F32),
        rs1=((R, 1), F32), n1=((L, D), BF16), q=((heads, L, HEAD_DIM), BF16),
        k=((heads, L, HEAD_DIM), BF16), v=((heads, L, HEAD_DIM), BF16), probs=((heads, L, L), BF16),
        heads=((heads, L, HEAD_DIM), BF16), mixed=((L, heads * HEAD_DIM), BF16),
        res2=((R, D), F32), xh2=((R, D), F32), rs2=((R, 1), F32), n2=((4 * R, D), BF16),
        hid=((4 * R, hidden), BF16), branch=((4 * R, D), BF16), preg=((4 * R, hidden), BF16),
        own=((2, R, D), F32), csend=((2, 2, R, D), BF16),
        crecv=((2, 2, R, D), BF16), xsend=((2, R, D), BF16), xrecv=((2, R, D), BF16),
        mb=((L, D), BF16), pg=((2, L, wide_in), BF16),
        sg=((2, L, channels), BF16), gtmp=((cin, channels), F32),
    )
    for name in ("up", "down"):
        scratch["g_" + name] = ((2,) + grads[name], BF16)
    for name in ("pin", "pout", "embed", "stem"):
        scratch["g_" + name] = ((2, 2) + grads[name], BF16)
    for name in ("pin", "pout", "embed", "stem"):
        scratch["x_" + name] = ((2,) + grads[name], BF16)
    order = ("up", "down", "pin", "pout", "embed", "stem")
    for name in order:
        scratch["y_" + name] = (grads[name], BF16)
    for name in order:
        scratch["z_" + name] = ((3, grads[name][0] // 4, grads[name][1]), BF16)
    for name in order:
        scratch["p_" + name] = ((grads[name][0] // 4, grads[name][1]), BF16)
    scratch.update(sm=((8, D), F32), smr=((3, 8, D), F32), smz=((4, 8, D), F32))
    copies = 96
    shapes = [pltpu.VMEM(*one) for one in scratch.values()]
    shapes += [pltpu.SemaphoreType.DMA((copies,)) for _ in range(2)]
    shapes += [pltpu.SemaphoreType.DMA((24,))]
    names = tuple(scratch) + ("send_sems", "recv_sems", "local_sems")
    results = pl.pallas_call(
        functools.partial(kernel, tuple(in_specs), tuple(outs), names),
        out_shape=[jax.ShapeDtypeStruct(shape, kind) for shape, kind, _ in outs.values()],
        in_specs=list(in_specs.values()),
        out_specs=[spec for _, _, spec in outs.values()],
        scratch_shapes=shapes,
        compiler_params=pltpu.CompilerParams(
            collective_id=0, has_side_effects=True, vmem_limit_bytes=62 * 2**20
        ),
        name="layer",
    )(
        features, stem_weight, group_gain, group_bias, embed_weight, first_gain, first_bias,
        project_in, project_out, second_gain, second_bias, up_weight, up_bias, down_weight,
        valid_mask, slot_slice, cotangent,
    )
    out = dict(zip(outs, results))

    wide = {name: out["o_" + name].astype(F32) for name in order}
    small = out["o_small"]
    bit = NEAR
    while bit < dp:
        pairs = [(i, i ^ bit) for i in range(dp)]
        wide, small = jax.tree.map(
            lambda part: part + lax.ppermute(part, "dp", pairs), (wide, small)
        )
        bit *= 2

    def rows_of(name):
        return wide[name].reshape(-1, wide[name].shape[-1])

    project_out_grad = jnp.moveaxis(wide["pout"], 0, 1).reshape(out_rows, D)
    return (
        out["block_out"],
        out["features_grad"],
        rows_of("stem"),
        small[5, 0:channels],
        small[5, channels : 2 * channels],
        rows_of("embed"),
        small[0],
        small[1],
        rows_of("pin"),
        project_out_grad,
        small[2],
        small[3],
        rows_of("up"),
        small[4],
        rows_of("down"),
    )


def solution(mesh):
    return jax.shard_map(
        functools.partial(body, dp=mesh.shape["dp"]),
        mesh=mesh,
        in_specs=(
            P("dp", None), P(None, "mp"), P("mp"), P("mp"), P("mp", None), P(), P(),
            P(None, "mp"), P("mp", None), P(), P(), P(None, "mp"), P("mp"), P("mp", None),
            P(), P("dp"), P(("dp", "mp"), None),
        ),
        out_specs=(
            P(("dp", "mp"), None), P(("dp", "mp"), None), P(None, "mp"), P("mp"), P("mp"),
            P("mp", None), P(), P(), P(None, "mp"), P("mp", None), P(), P(), P(None, "mp"),
            P("mp"), P("mp", None),
        ),
        check_vma=False,
    )
```

time: 824 us -> 243 us (0.29)
  waiting for transfers between devices: 503 us -> 0 us
  Pallas kernels: 0 us -> 224 us
  matrix products: 83.4 us -> 0 us
  local copies, waits for them, and re-layouts: 88 us -> 8.01 us
  blocking collectives: 66.5 us -> 0 us
  other arithmetic: 58.9 us -> 6.54 us
  between operations: 15.2 us -> 0.7 us
    pallas_call x0 -> x1, Pallas kernels: none -> 224 us  [body(): pl.pallas_call(functools.partial(kernel, tuple(in_specs), tuple(outs), na...]
    psum x1 -> x0, waiting for transfers between devices: 217 us -> none  [body(): lax.psum((stem_weight_grad, group_gain_grad, group_bias_grad, embed_weigh...]
    reduce_scatter x6 -> x0, waiting for transfers between devices: 211 us -> none  [the longest x3 131 us: narrow_product(): lax.psum_scatter(plain_or_transposed(block_in, weight, transposed), 'mp',...]
    dot_general x32 -> x0, matrix products: 83.4 us -> none  [the longest x6 30.2 us: times_transposed(): lax.dot_general(left, right, (((1,), (1,)), ((), ())), preferred_element_...]
    all_gather x5 -> x0, waiting for transfers between devices: 75.4 us -> none  [the longest x1 20.7 us: body(): lax.all_gather(second_grad.astype(jnp.bfloat16), 'mp', axis=0, tiled=True)]
    psum x2 -> x0, blocking collectives: 66.5 us -> none  [the longest x1 43.8 us: body(): lax.psum((first_gain_grad, first_bias_grad, second_gain_grad, second_bias...]
    reduce_sum x19 -> x0, other arithmetic: 26.3 us -> none  [the longest x1 5.98 us: group_norm(): centered * lax.rsqrt(variance + 1e-05)]
    convert_element_type x9 -> x0, other arithmetic: 18.7 us -> none  [the longest x1 5.48 us: body(): activated_low = activated.astype(jnp.bfloat16)]
  transfers between devices with their start and end apart: 12 -> 0, of which waited for: 11 -> 0; matrix products, arithmetic and copies ran while one was open for 6% -> 0% of each run, Pallas kernels for 0% -> 0%
where the time goes in v1:
time: 243 us; the launch traced here: 239 us
  Pallas kernels  224 us (92%)
  local copies, waits for them, and re-layouts  8.01 us (3%)
  other arithmetic  6.54 us (3%)
    pallas_call x1, Pallas kernels, body(): pl.pallas_call(functools.partial(kernel, tuple(in_specs), tuple(outs), na...  224 us
    reshape x4, other arithmetic, rows_of(): return wide[name].reshape(-1, wide[name].shape[-1])  6.5 us
    unnamed x18, local copies, waits for them, and re-layouts  5.95 us

profile of v1, /device:TPU:0, one launch (start us, length us, event | category | flops | bytes accessed | tf_op | source)
XLA Modules:
  0.0 239.2 jit_solution(3410625240613892601)
XLA Ops:
  0.6 2.2 copy.34.refs_7_
  2.9 224.0 %layer.1 = (bf16[288,768]{1,0:T(8,128)(2,1)}, f32[288,1024]{1,0:T(8,128)}, bf16[2,512,256]{2,1,0:T(8,128)(2,1)}, bf16[2,128,768]{2,1,0:T(8,128)(2,1)}, bf16[2,38...) custom-call(bf16[1152,1024]{1,0:T(8,128)(2,1)} %refs_0_.1, ...), custom_call_target="tpu_custom_call" | custom-call | tf_op jit(solution)/shard_map/layer/pallas_call | solution.py:750
  226.8 0.0 copy-start.6
  226.9 0.0 copy-start.1
  226.9 4.3 %bitcast_convert_fusion = (f32[768,768]{1,0:T(8,128)}, f32[768,768]{1,0:T(8,128)}) fusion(bf16[2,384,768]{2,1,0:T(8,128)(2,1)} %get-tuple-element.32, bf16[2,384,768]{2,1,0:T(8,128)(2,1)} %get-tuple-element.31), kind=kLoop, calls=%fused_computation | loop fusion | flops 1179648 | bytes 7077888 | tf_op jit(solution)/shard_map/reshape | solution.py:778
  231.1 0.0 copy-done.6
  231.1 0.6 slice_reduce_fusion
  231.8 0.6 fusion
  232.3 0.0 copy-done.1
  232.3 0.2 bitcast_convert_fusion.2
  232.5 0.0 copy-start.5
  232.6 1.7 copy.36
  234.3 0.0 copy-start.2
  234.3 0.0 copy-done.5
  234.3 0.0 copy-start.4
  234.3 0.0 copy-start.3
  234.3 0.9 copy.37
  235.2 0.2 copy-done.2
  235.4 0.0 copy-start
  235.4 1.1 bitcast_convert_fusion.3
  236.5 0.0 copy-done.4
  236.5 1.0 bitcast_convert_fusion.4
  237.4 0.0 copy-done.3
  237.4 0.8 copy.40
  238.2 0.0 copy-done
  238.2 1.0 copy.41
  (1 shorter events, 0.0 us)
Async XLA Ops:
  226.8 4.3 %copy-start.6 = (f32[8,768]{1,0:T(8,128)S(1)}, f32[8,768]{1,0:T(8,128)}, u32[]{:S(2)}) copy-start(f32[8,768]{1,0:T(8,128)} %get-tuple-element.27) | copy-start | bytes 73732
  226.9 5.5 %copy-start.1 = (bf16[2,384,576]{2,1,0:T(8,128)(2,1)S(1)}, bf16[2,384,576]{2,1,0:T(8,128)(2,1)}, u32[]{:S(2)}) copy-start(bf16[2,384,576]{2,1,0:T(8,128)(2,1)} %get-tuple-element.29) | copy-start | bytes 2654212
  232.5 1.7 copy-start.5
  234.3 1.1 copy-start.2
  234.3 2.2 copy-start.4
  234.3 3.1 %copy-start.3 = (bf16[288,768]{1,0:T(8,128)(2,1)S(1)}, bf16[288,768]{1,0:T(8,128)(2,1)}, u32[]{:S(2)}) copy-start(bf16[288,768]{1,0:T(8,128)(2,1)} %get-tuple-element.87) | copy-start | bytes 1327108
  235.4 2.8 %copy-start = (f32[288,1024]{1,0:T(8,128)S(1)}, f32[288,1024]{1,0:T(8,128)}, u32[]{:S(2)}) copy-start(f32[288,1024]{1,0:T(8,128)} %get-tuple-element.88) | copy-start | bytes 3538948

commit v2 on v1

--- a/solution.py
+++ b/solution.py
@@ -65,64 +65,75 @@
 
 
 class Summed:
-    def __init__(self, net, place, grad, half_in, parts_in, piece, out):
-        self.net, self.place = net, place
-        self.grad, self.half_in, self.parts_in, self.piece, self.out = (
-            grad,
-            half_in,
-            parts_in,
-            piece,
-            out,
+    def __init__(self, net, place, order, grad, arrive, piece, out, far=None, far_in=None):
+        self.net, self.place, self.order = net, place, order
+        self.grad, self.arrive, self.piece, self.out = grad, arrive, piece, out
+        self.far, self.far_in = far, far_in
+        self.at, self.size, self.slot = 0, grad.shape[0], 0
+        self.level, self.back = 0, False
+
+    def send_far(self):
+        self.copy = self.net.send(self.far, self.far_in, self.place.far)
+
+    def add(self, at, source, count):
+        for t in range(count):
+            self.grad[at + t] = (
+                self.grad[at + t].astype(F32) + source(t).astype(F32)
+            ).astype(BF16)
+
+    def start(self):
+        bit, partner = self.place.partner(self.order[self.level])
+        half = self.size // 2
+        give = pl.ds(self.at + (1 - bit) * half, half)
+        self.at = self.at + bit * half
+        self.copy = self.net.send(
+            self.grad.at[give], self.arrive.at[pl.ds(self.slot, half)], partner
         )
-        self.rows = grad.shape[-2]
-        self.part = self.rows // 4
-
-    def start(self):
-        y = self.place.y
-        self.half = self.net.send(self.grad.at[1 - y], self.half_in, self.place.y_device)
-
-    def spread(self):
-        y, zi = self.place.y, self.place.zi
-        self.half.wait_recv()
-        for t in range(4):
-            rows = pl.ds(t * self.part, self.part)
-            self.grad[y, rows, :] = (
-                self.grad[y, rows, :].astype(F32) + self.half_in[rows, :].astype(F32)
-            ).astype(BF16)
-        self.parts = []
-        for k in range(1, 4):
-            to = lax.rem(zi + k, 4)
-            rows = pl.ds(pl.multiple_of(to * self.part, 16), self.part)
-            self.parts.append(
-                self.net.send(
-                    self.grad.at[y, rows], self.parts_in.at[k - 1], self.place.z_device(k)
-                )
-            )
-
-    def gather(self):
-        y, zi = self.place.y, self.place.zi
-        rows = pl.ds(pl.multiple_of(zi * self.part, 16), self.part)
-        for copy in self.parts:
-            copy.wait_recv()
-        total = self.grad[y, rows, :].astype(F32)
-        for k in range(3):
-            total = total + self.parts_in[k].astype(F32)
-        self.piece[...] = total.astype(BF16)
-        target = self.out.at[y, rows]
-        self.own = self.net.local(self.piece, target)
-        self.pieces = [
-            self.net.send(self.piece, target, self.place.z_device(k)) for k in range(1, 4)
-        ]
 
     def share(self):
-        y = self.place.y
-        self.own.wait()
-        for copy in self.pieces:
-            copy.wait_recv()
-        self.last = self.net.send(self.out.at[y], self.out.at[y], self.place.y_device)
-
-    def done(self):
-        self.last.wait_recv()
+        held = pl.ds(self.at, self.size)
+        bit, partner = self.place.partner(self.order[self.level])
+        self.copy = self.net.send(self.out.at[held], self.out.at[held], partner)
+        self.at = self.at - bit * self.size
+
+    def step(self):
+        self.copy.wait_recv()
+        if self.far is not None:
+            self.far = None
+            self.add(0, lambda t: self.far_in[t], self.size)
+            self.start()
+        elif not self.back:
+            half = self.size // 2
+            slot = self.slot
+            self.size, self.slot = half, slot + half
+            self.level += 1
+            if self.level < len(self.order):
+                self.add(self.at, lambda t: self.arrive[slot + t], half)
+                self.start()
+            else:
+                self.back = True
+                self.level -= 1
+                self.piece[0] = (
+                    self.grad[self.at].astype(F32) + self.arrive[slot].astype(F32)
+                ).astype(BF16)
+                held = pl.ds(self.at, 1)
+                self.own = self.net.local(self.piece, self.out.at[held])
+                bit, partner = self.place.partner(self.order[self.level])
+                self.copy = self.net.send(self.piece, self.out.at[held], partner)
+                self.at = self.at - bit
+        else:
+            if self.size == 1:
+                self.own.wait()
+            self.size *= 2
+            self.level -= 1
+            if self.level >= 0:
+                self.share()
+                return
+            self.copy = None
+
+    def step_all(self):
+        while self.copy is not None:
+            self.step()
 
 
 class Place:
@@ -133,7 +144,7 @@
         self.c = lax.rem(self.m, 2)
         self.y = lax.rem(self.d, 2)
         self.zi = lax.div(lax.rem(self.d, NEAR), 2)
-        self.base = self.d - lax.rem(self.d, NEAR)
+        self.bits = {"y": (self.y, 1), "a": (lax.rem(self.zi, 2), 2), "b": (lax.div(self.zi, 2), 4)}
         self.sib_m = self.m + 1 - 2 * self.c
         self.far_m = lax.rem(self.m + 2, 4)
         self.far_sib_m = lax.rem(self.sib_m + 2, 4)
@@ -141,30 +152,45 @@
         self.far = (self.d, self.far_m)
         self.y_device = (self.d + 1 - 2 * self.y, self.m)
 
-    def z_device(self, k):
-        return (self.base + 2 * lax.rem(self.zi + k, 4) + self.y, self.m)
+    def partner(self, name):
+        bit, stride = self.bits[name]
+        return bit, (self.d + stride - 2 * stride * bit, self.m)
+
+
+GRADS = ("up", "down", "pout", "pin0", "pin1", "pin2", "embed", "stem")
+BY_SLOT = GRADS[2:]
+KINDS = dict(g="grad", f="far", i="far_in", r="arrive", p="piece", o="out")
+ORDER = (
+    "norm2", "mixed_back", "heads_far", "down", "up", "heads_own", "norm1_send", "down", "up",
+    "norm1", "pout", "stem_far", "stem_own", "down", "up", "features_send", "pin0", "pout",
+    "features_sum", "small", "result", "down", "up", "pout", "pin0", "embed", "small", "down",
+    "up", "pin0", "pout", "embed", "small", "stem", "pout", "pin0", "embed", "small", "stem",
+    "pout", "pin0", "pin1", "small", "embed", "stem", "pin0", "pin1", "pin2", "embed", "stem",
+    "pin1", "pin2", "embed", "stem", "pin1", "pin2", "stem", "pin1", "pin2", "stem", "pin1",
+    "pin2", "pin1", "pin2",
+)
 
 
 def kernel(in_names, out_names, scratch_names, *refs):
     names = in_names + out_names + scratch_names
     r = dict(zip(names, refs))
-    run(**r)
+    sums = {name: {} for name in GRADS}
+    for name in names:
+        kind, _, which = name.partition("_")
+        if which in sums and kind in KINDS:
+            sums[which][KINDS[kind]] = r.pop(name)
+    run(sums=sums, **r)
 
 
 def run(
     features, stem_weight, group_gain, group_bias, embed_weight, first_gain, first_bias,
     project_in, project_out, second_gain, second_bias, up_weight, up_bias, down_weight,
     valid_mask, slot_slice, cotangent,
-    block_out, features_grad, o_stem, o_embed, o_pin, o_pout, o_up, o_down, o_small,
+    block_out, features_grad, o_small,
     feat, stem, std, wstat, embed, pin, pout, up, down, gvec, xhs, dgs, act, gst,
     sbuf, rbuf, res1, xh1, rs1, n1, q, k, v, probs, heads, mixed, res2, xh2, rs2,
     n2, hid, branch, preg, own, csend, crecv, xsend, xrecv, mb, pg, sg, gtmp,
-    g_up, g_down, g_pin, g_pout, g_embed, g_stem,
-    x_pin, x_pout, x_embed, x_stem,
-    y_up, y_down, y_pin, y_pout, y_embed, y_stem,
-    z_up, z_down, z_pin, z_pout, z_embed, z_stem,
-    p_up, p_down, p_pin, p_pout, p_embed, p_stem,
-    sm, smr, smz, send_sems, recv_sems, local_sems,
+    sm, smr, send_sems, recv_sems, local_sems, sums,
 ):
     place = Place()
     net = Net(send_sems, recv_sems, local_sems)
@@ -179,7 +205,7 @@
         return pl.ds(pl.multiple_of(m * R, 16), R)
 
     barrier = pltpu.get_barrier_semaphore()
-    peers = [place.sib, place.far, place.y_device] + [place.z_device(i) for i in (1, 2, 3)]
+    peers = [place.sib, place.far] + [place.partner(name)[1] for name in place.bits]
     for peer in peers:
         pl.semaphore_signal(barrier, inc=1, device_id=peer, device_id_type=MESH)
     l_stem = net.local(stem_weight, stem.at[0])
@@ -195,7 +221,25 @@
     pl.semaphore_wait(barrier, len(peers))
 
     c_gvec = net.send(gvec.at[0], gvec.at[1], place.far)
-    c_stem = net.send(stem_weight, stem.at[1], place.far)
+
+    def halves(weight, kept, pieces):
+        rows = weight.shape[0] // 2 // pieces
+        for t in range(pieces):
+            at = pl.ds(pl.multiple_of((place.y * pieces + t) * rows, 16), rows)
+            yield kept.at[1, at], net.send(weight.at[at], kept.at[1, at], place.far)
+
+    stem_half = list(halves(stem_weight, stem, 2))
+    embed_half = list(halves(embed_weight, embed, 1))
+    pin_half = list(halves(project_in, pin, 2))
+    pout_half = list(halves(project_out, pout, 1))
+    c_cot = [
+        net.send(cotangent, branch.at[block(place.m)], device) for device in (place.far, place.sib)
+    ]
+
+    def pass_on(half):
+        ref, copy = half
+        copy.wait_recv()
+        return net.send(ref, ref, place.y_device)
 
     slices = valid_mask.shape[0]
     lengths = jnp.sum(valid_mask[...].astype(F32), axis=1, keepdims=True)
@@ -258,17 +302,18 @@
 
     l_stem.wait()
     standardize(0)
+    c_stem = [pass_on(stem_half[0])]
     l_feat.wait()
     stem_forward(0)
-    c_embed = net.send(embed_weight, embed.at[1], place.far)
+    c_stem.append(pass_on(stem_half[1]))
     c_gvec.wait_recv()
-    c_stem.wait_recv()
+    c_embed = pass_on(embed_half[0])
+    for copy in c_stem:
+        copy.wait_recv()
     standardize(1)
-    c_pin = net.send(project_in, pin.at[1], place.far)
     stem_forward(1)
     l_embed.wait()
     c_embed.wait_recv()
-    c_pout = net.send(project_out, pout.at[1], place.far)
 
     def core_sum(product):
         width = pl.ds(0, D)
@@ -303,16 +348,18 @@
             scale_ref[rows, :] = scale
             out_ref[pl.ds(out_start + t * step, step), :] = (xh * gain + bias).astype(BF16)
 
+    c_pin = [pass_on(pin_half[0])]
     layer_norm(res1, rbuf, None, first_gain, first_bias, xh1, rs1, n1, own_rows)
     c_n1 = net.send(n1.at[pl.ds(own_rows, R)], n1.at[pl.ds(own_rows, R)], place.sib)
     l_pin.wait()
     c_n1.wait_recv()
-
-    per_shard = pin.shape[2] // (3 * HEAD_DIM)
+    c_pin.append(pass_on(pin_half[1]))
+
+    per_shard = pin.shape[1] // (3 * HEAD_DIM)
 
     def attend(j):
         for at, size in tile_rows:
-            packed = dot(n1[at : at + size, :], pin[j]).astype(BF16)
+            packed = dot(n1[at : at + size, :], pin[j], 1, 1).astype(BF16)
             for h in range(per_shard):
                 for i, ref in enumerate((q, k, v)):
                     lane = (3 * h + i) * HEAD_DIM
@@ -331,10 +378,9 @@
         lax.fori_loop(0, per_shard, head, 0)
 
     attend(0)
-    c_pin.wait_recv()
-    c_cot = [
-        net.send(cotangent, branch.at[block(place.m)], device) for device in (place.far, place.sib)
-    ]
+    c_pout = pass_on(pout_half[0])
+    for copy in c_pin:
+        copy.wait_recv()
     attend(1)
 
     def side_by_side(pieces, store):
@@ -440,26 +486,30 @@
     xsend[0] = (sbuf[:, 0:D] + crecv[0, 1].astype(F32)).astype(BF16)
     c_far[0] = net.send(xsend.at[0], xrecv.at[0], place.far)
 
-    summed = {
-        "down": Summed(net, place, g_down, y_down, z_down, p_down, o_down),
-        "up": Summed(net, place, g_up, y_up, z_up, p_up, o_up),
-        "pout": Summed(net, place, g_pout.at[0], y_pout, z_pout, p_pout, o_pout),
-        "pin": Summed(net, place, g_pin.at[0], y_pin, z_pin, p_pin, o_pin),
-        "embed": Summed(net, place, g_embed.at[0], y_embed, z_embed, p_embed, o_embed),
-        "stem": Summed(net, place, g_stem.at[0], y_stem, z_stem, p_stem, o_stem),
-    }
+    def make(name, order):
+        return Summed(net, place, order, **sums[name])
+
+    summed = {name: make(name, "ayb" if name == "up" else "yab") for name in GRADS}
+
+    def keep(name, which, at, value):
+        ref = sums[name][which]
+        rows = ref.shape[1]
+        count = value.shape[0] // rows
+        ref[at : at + count] = value.reshape(count, rows, value.shape[1]).astype(BF16)
 
     half = D // 2
     for i in range(2):
-        g_down[i] = dot(hid[:, i * half : (i + 1) * half], branch[...], 0, 0).astype(BF16)
+        value = dot(hid[:, i * half : (i + 1) * half], branch[...], 0, 0)
+        keep("down", "grad", 4 * i, value)
     summed["down"].start()
     for i in range(2):
-        g_up[i] = dot(n2[:, i * half : (i + 1) * half], preg[...], 0, 0).astype(BF16)
+        value = dot(n2[:, i * half : (i + 1) * half], preg[...], 0, 0)
+        keep("up", "grad", 4 * i, value)
     summed["up"].start()
     sm[...] = jnp.zeros_like(sm)
     sm[4:5, :] = bias_sum[0] + bias_sum[1] + bias_sum[2] + bias_sum[3]
 
-    def norm_back(grad_of, gain, xh_ref, scale_ref, keep, out_ref, out_start, row):
+    def norm_back(grad_of, gain, xh_ref, scale_ref, kept, out_ref, out_start, row):
         gain = gain[...].reshape(1, -1)
         gain_sum = jnp.zeros((1, D), F32)
         bias_total = jnp.zeros((1, D), F32)
@@ -473,52 +523,66 @@
             mean_one = jnp.sum(dy, axis=1, keepdims=True) * (1.0 / D)
             mean_two = jnp.sum(dy * xh, axis=1, keepdims=True) * (1.0 / D)
             dx = through + scale_ref[rows, :] * (dy - mean_one - xh * mean_two)
-            if keep is not None:
-                keep[rows, :] = dx
+            if kept is not None:
+                kept[rows, :] = dx
             out_ref[pl.ds(out_start + t * step, step), :] = dx.astype(BF16)
         sm[row : row + 1, :] = gain_sum
         sm[row + 1 : row + 2, :] = bias_total
 
+    own_part = pl.ds(own_rows, R)
     sg2, eb = res1, mb
-    c_core[1, 0].wait_recv()
-    c_far[1].wait_recv()
-
-    def second_grad_of(rows):
-        dy = own[1, rows, :] + crecv[1, 0, rows, :].astype(F32) + xrecv[1, rows, :].astype(F32)
-        at = pl.ds(pl.multiple_of(place.m * R, 16) + rows.start, step)
-        return dy, branch[at, :].astype(F32)
-
-    norm_back(second_grad_of, second_gain, xh2, rs2, sg2, mb, own_rows, 2)
-    c_mb = net.send(mb.at[pl.ds(own_rows, R)], mb.at[pl.ds(own_rows, R)], place.sib)
-
-    c_core[0, 0].wait_recv()
-    c_far[0].wait_recv()
-    net.sent(c_core[0, 0])
-    for t in range(3):
-        rows = slice(t * step, (t + 1) * step)
-        value = (
-            res2[rows, :]
-            + own[0, rows, :]
-            + crecv[0, 0, rows, :].astype(F32)
-            + xrecv[0, rows, :].astype(F32)
-        )
-        csend[0, 0, rows, :] = (value * valid_rows(own_rows + t * step, step)).astype(BF16)
-    l_bout = net.local(csend.at[0, 0], block_out)
-
-    c_mb.wait_recv()
-    grad = dot(mixed[...], mb[...], 0, 0)
-    shard = pout.shape[1]
-    wide = g_pout.shape[3]
-    for j in (1, 0):
-        for i in range(2):
-            g_pout[j, i] = grad[j * shard : (j + 1) * shard, i * wide : (i + 1) * wide].astype(BF16)
-    cx = {}
-    cx["pout"] = net.send(g_pout.at[1], x_pout, place.far)
+    copies = {}
+    locals_left = []
+    tasks = {}
+
+    def task(function):
+        tasks[function.__name__] = function
+
+    @task
+    def norm2():
+        c_core[1, 0].wait_recv()
+        c_far[1].wait_recv()
+
+        def grad_of(rows):
+            dy = own[1, rows, :] + crecv[1, 0, rows, :].astype(F32) + xrecv[1, rows, :].astype(F32)
+            at = pl.ds(pl.multiple_of(place.m * R, 16) + rows.start, step)
+            return dy, branch[at, :].astype(F32)
+
+        norm_back(grad_of, second_gain, xh2, rs2, sg2, mb, own_rows, 2)
+        copies["mb"] = net.send(mb.at[own_part], mb.at[own_part], place.sib)
+
+    @task
+    def result():
+        c_core[0, 0].wait_recv()
+        c_far[0].wait_recv()
+        net.sent(c_core[0, 0])
+        for t in range(3):
+            rows = slice(t * step, (t + 1) * step)
+            value = (
+                res2[rows, :]
+                + own[0, rows, :]
+                + crecv[0, 0, rows, :].astype(F32)
+                + xrecv[0, rows, :].astype(F32)
+            )
+            csend[0, 0, rows, :] = (value * valid_rows(own_rows + t * step, step)).astype(BF16)
+        locals_left.append(net.local(csend.at[0, 0], block_out))
+
     whole_out = jnp.concatenate([pout[0], pout[1]], axis=0)
-    for at, size in tile_rows:
-        value = dot(mb[at : at + size, :], whole_out, 1, 1).astype(BF16)
-        for h in range(2 * per_shard):
-            heads[h, at : at + size, :] = value[:, h * HEAD_DIM : (h + 1) * HEAD_DIM]
+
+    @task
+    def mixed_back():
+        copies["mb"].wait_recv()
+        value = dot(mixed[...], mb[...], 0, 0)
+        shard = pout.shape[1]
+        for j, which in ((1, "far"), (0, "grad")):
+            rows = value[j * shard : (j + 1) * shard]
+            for i in range(2):
+                keep("pout", which, 4 * i, rows[:, i * half : (i + 1) * half])
+        summed["pout"].send_far()
+        for at, size in tile_rows:
+            value = dot(mb[at : at + size, :], whole_out, 1, 1).astype(BF16)
+            for h in range(2 * per_shard):
+                heads[h, at : at + size, :] = value[:, h * HEAD_DIM : (h + 1) * HEAD_DIM]
 
     def head_back(h, carry):
         p = probs[h]
@@ -531,53 +595,57 @@
         q[h] = dq
         return carry
 
-    lax.fori_loop(0, 2 * per_shard, head_back, 0)
-
-    for j in (1, 0):
+    def pin_back(j, which):
+        lax.fori_loop(per_shard * j, per_shard * (j + 1), head_back, 0)
 
         def store_pg(lanes, value):
             pg[j, :, lanes] = value
 
         pieces = [ref[per_shard * j + h] for h in range(per_shard) for ref in (q, k, v)]
         side_by_side(pieces, store_pg)
-    for j in (1, 0):
-        for i in range(2):
-            g_pin[j, i] = dot(n1[:, i * half : (i + 1) * half], pg[j], 0, 0).astype(BF16)
-        if j == 1:
-            cx["pin"] = net.send(g_pin.at[1], x_pin, place.far)
-
-    def first_product(start):
-        rows = pl.ds(start, R)
-        return dot(pg[0, rows, :], pin[0], 1, 1) + dot(pg[1, rows, :], pin[1], 1, 1)
-
-    own[0] = core_sum(first_product)
-
-    def first_grad_of(rows):
-        return own[0, rows, :] + rbuf[rows, 0:D], sg2[rows, :]
-
-    net.sent(c_mb)
-    norm_back(first_grad_of, first_gain, xh1, rs1, None, eb, own_rows, 0)
-    c_eb = net.send(eb.at[pl.ds(own_rows, R)], eb.at[pl.ds(own_rows, R)], place.sib)
-
-    def far_sum(name, grad, arrived):
-        cx[name].wait_recv()
-        for i in range(2):
-            grad[0, i] = (grad[0, i].astype(F32) + arrived[i].astype(F32)).astype(BF16)
-        summed[name].start()
-
-    summed["down"].spread()
-    far_sum("pout", g_pout, x_pout)
-    c_eb.wait_recv()
-
-    embed_half = embed.shape[1] // 2
-    for j in (1, 0):
-        grad = dot(act[j], eb[...], 0, 0)
-        for i in range(2):
-            g_embed[j, i] = grad[i * embed_half : (i + 1) * embed_half, :].astype(BF16)
-        if j == 1:
-            cx["embed"] = net.send(g_embed.at[1], x_embed, place.far)
+        value = dot(pg[j], n1[...], 0, 0)
+        wide = D // 6
+        for i in range(6):
+            keep("pin%d" % (i // 2), which, 4 * (i % 2), value[:, i * wide : (i + 1) * wide])
+
+    @task
+    def heads_far():
+        pin_back(1, "far")
+        summed["pin0"].send_far()
+
+    @task
+    def heads_own():
+        pin_back(0, "grad")
+
+    @task
+    def norm1_send():
+        def product(start):
+            rows = pl.ds(start, R)
+            return dot(pg[0, rows, :], pin[0]) + dot(pg[1, rows, :], pin[1])
+
+        width = pl.ds(0, D)
+        sbuf[:, width] = product(sib_rows)
+        copies["n1"] = net.send(sbuf.at[:, width], rbuf.at[:, width], place.sib)
+        xh2[...] = product(own_rows)
+
+    @task
+    def norm1():
+        copies["n1"].wait_recv()
+        net.sent(copies["n1"])
+
+        def grad_of(rows):
+            return xh2[rows, :] + rbuf[rows, 0:D], sg2[rows, :]
+
+        net.sent(copies["mb"])
+        norm_back(grad_of, first_gain, xh1, rs1, None, eb, own_rows, 0)
+        copies["eb"] = net.send(eb.at[own_part], eb.at[own_part], place.sib)
+
+    def embed_back(j, which):
+        keep("embed", which, 0, dot(act[j], eb[...], 0, 0))
+
     cin = feat.shape[1]
-    for j in (1, 0):
+
+    def stem_back(j, which):
         gain_sum = jnp.zeros((1, channels), F32)
         bias_total = jnp.zeros((1, channels), F32)
         for at, size in tile_rows:
@@ -612,67 +680,75 @@
         for t in range(4):
             rows = slice(t * quarter, (t + 1) * quarter)
             xh = (stem[j, rows, :].astype(F32) - average) * scale
-            value = (gtmp[rows, :] - sum_one - xh * sum_two) * scale
-            g_stem[j, t // 2, (t % 2) * quarter : (t % 2 + 1) * quarter, :] = value.astype(BF16)
-        if j == 1:
-            cx["stem"] = net.send(g_stem.at[1], x_stem, place.far)
-
-    c_sm = net.send(sm, smr.at[0], place.sib)
-    summed["up"].spread()
-    summed["down"].gather()
-    far_sum("pin", g_pin, x_pin)
-    c_sm.wait_recv()
-    net.sent(c_sm)
-    sm[0:4, :] = sm[0:4, :] + smr[0, 0:4, :]
-    c_sm = net.send(sm, smr.at[1], place.far)
-
-    def feature_product(start):
-        rows = pl.ds(start, R)
-        return dot(sg[0, rows, :], std[0], 1, 1) + dot(sg[1, rows, :], std[1], 1, 1)
-
-    sbuf[...] = feature_product(sib_rows)
-    c_feat = net.send(sbuf, rbuf, place.sib)
-    mine_feat = feature_product(own_rows)
-    c_feat.wait_recv()
-    net.sent(c_feat)
-    sbuf[...] = mine_feat + rbuf[...]
-    l_fgrad = net.local(sbuf, features_grad)
-
-    far_sum("embed", g_embed, x_embed)
-    c_sm.wait_recv()
-    net.sent(c_sm)
-    sm[0:4, :] = sm[0:4, :] + smr[1, 0:4, :]
-    sm[5:6, :] = sm[5:6, :] + smr[1, 6:7, :]
-    c_sm = net.send(sm, smr.at[2], place.y_device)
-    summed["pout"].spread()
-    summed["up"].gather()
-    far_sum("stem", g_stem, x_stem)
-    summed["down"].share()
-    c_sm.wait_recv()
-    net.sent(c_sm)
-    smz[place.zi] = sm[...] + smr[2]
-    c_smz = [
-        net.send(smz.at[place.zi], smz.at[place.zi], place.z_device(i)) for i in (1, 2, 3)
-    ]
-    summed["pout"].gather()
-    summed["pin"].spread()
-    summed["up"].share()
-    summed["embed"].spread()
-    summed["pin"].gather()
-    summed["pout"].share()
-    summed["stem"].spread()
-    for copy in c_smz:
-        copy.wait_recv()
-    o_small[...] = smz[0] + smz[1] + smz[2] + smz[3]
-    summed["embed"].gather()
-    summed["pin"].share()
-    summed["stem"].gather()
-    summed["embed"].share()
-    summed["stem"].share()
-    l_bout.wait()
-    l_fgrad.wait()
+            keep("stem", which, 2 * t, (gtmp[rows, :] - sum_one - xh * sum_two) * scale)
+
+    @task
+    def stem_far():
+        copies["eb"].wait_recv()
+        embed_back(1, "far")
+        summed["embed"].send_far()
+        stem_back(1, "far")
+        for name in ("stem", "pin1", "pin2"):
+            summed[name].send_far()
+
+    @task
+    def stem_own():
+        embed_back(0, "grad")
+        stem_back(0, "grad")
+        small("core")
+
+    @task
+    def features_send():
+        def product(start):
+            rows = pl.ds(start, R)
+            return dot(sg[0, rows, :], std[0], 1, 1) + dot(sg[1, rows, :], std[1], 1, 1)
+
+        sbuf[...] = product(sib_rows)
+        copies["feat"] = net.send(sbuf, rbuf, place.sib)
+        copies["feat_own"] = product(own_rows)
+
+    @task
+    def features_sum():
+        copies["feat"].wait_recv()
+        net.sent(copies["feat"])
+        sbuf[...] = copies["feat_own"] + rbuf[...]
+        locals_left.append(net.local(sbuf, features_grad))
+
+    small_at = {"core": place.sib, "x": place.far}
+    for name in place.bits:
+        small_at[name] = place.partner(name)[1]
+    small_order = tuple(small_at)
+
+    def small(name):
+        copies["small"] = net.send(sm, smr.at[small_order.index(name)], small_at[name])
+
+    def small_step(i):
+        copies["small"].wait_recv()
+        net.sent(copies["small"])
+        if small_order[i] in ("core", "x"):
+            sm[0:4, :] = sm[0:4, :] + smr[i, 0:4, :]
+            if small_order[i] == "x":
+                sm[5:6, :] = sm[5:6, :] + smr[i, 6:7, :]
+        else:
+            sm[...] = sm[...] + smr[i]
+        if i + 1 < len(small_order):
+            small(small_order[i + 1])
+        else:
+            o_small[...] = sm[...]
+
+    small_next = list(range(len(small_order)))
+    for name in ORDER:
+        if name in tasks:
+            tasks.pop(name)()
+        elif name == "small":
+            small_step(small_next.pop(0))
+        else:
+            summed[name].step()
+    assert not tasks and not small_next
     for one in summed.values():
-        one.done()
+        one.step_all()
+    for copy in locals_left:
+        copy.wait()
     net.finish()
 
 
@@ -687,6 +763,7 @@
     cin, channels = stem_weight.shape
     D = cotangent.shape[1]
     wide_in = project_in.shape[1]
+    project_in = project_in.T
     out_rows = project_out.shape[0]
     hidden = up_weight.shape[1]
     heads = 2 * wide_in // (3 * HEAD_DIM)
@@ -699,21 +776,26 @@
         second_bias=vmem, up_weight=hbm, up_bias=vmem, down_weight=hbm, valid_mask=vmem,
         slot_slice=smem, cotangent=hbm,
     )
-    grads = dict(
-        up=(D // 2, hidden),
-        down=(hidden // 2, D),
-        pin=(D // 2, wide_in),
-        pout=(out_rows, D // 2),
-        embed=(channels // 2, D),
-        stem=(cin // 2, channels),
-    )
-    outs = dict(block_out=((R, D), BF16, hbm), features_grad=((R, cin), F32, hbm))
-    for name in ("stem", "embed", "pin", "pout", "up", "down"):
-        outs["o_" + name] = ((2,) + grads[name], BF16, hbm)
-    outs["o_small"] = ((8, D), F32, vmem)
+    parts = dict(
+        up=(D // 8, hidden),
+        down=(hidden // 8, D),
+        pout=(out_rows // 4, D // 2),
+        pin0=(wide_in // 4, D // 6),
+        pin1=(wide_in // 4, D // 6),
+        pin2=(wide_in // 4, D // 6),
+        embed=(channels // 8, D),
+        stem=(cin // 8, channels),
+    )
+    outs = dict(
+        block_out=((R, D), BF16, hbm),
+        features_grad=((R, cin), F32, hbm),
+        o_small=((8, D), F32, vmem),
+    )
+    for name in GRADS:
+        outs["o_" + name] = ((8,) + parts[name], BF16, hbm)
     scratch = dict(
         feat=((L, cin), BF16), stem=((2, cin, channels), BF16), std=((2, cin, channels), BF16),
-        wstat=((2, 8, channels), F32), embed=((2, channels, D), BF16), pin=((2, D, wide_in), BF16),
+        wstat=((2, 8, channels), F32), embed=((2, channels, D), BF16), pin=((2, wide_in, D), BF16),
         pout=((2, out_rows, D), BF16), up=((D, hidden), BF16), down=((hidden, D), BF16),
         gvec=((2, 8, channels), F32), xhs=((2, L, channels), F32), dgs=((2, L, channels), F32),
         act=((2, L, channels), BF16), gst=((2, 8, channels), F32),
@@ -728,21 +810,13 @@
         mb=((L, D), BF16), pg=((2, L, wide_in), BF16),
         sg=((2, L, channels), BF16), gtmp=((cin, channels), F32),
     )
-    for name in ("up", "down"):
-        scratch["g_" + name] = ((2,) + grads[name], BF16)
-    for name in ("pin", "pout", "embed", "stem"):
-        scratch["g_" + name] = ((2, 2) + grads[name], BF16)
-    for name in ("pin", "pout", "embed", "stem"):
-        scratch["x_" + name] = ((2,) + grads[name], BF16)
-    order = ("up", "down", "pin", "pout", "embed", "stem")
-    for name in order:
-        scratch["y_" + name] = (grads[name], BF16)
-    for name in order:
-        scratch["z_" + name] = ((3, grads[name][0] // 4, grads[name][1]), BF16)
-    for name in order:
-        scratch["p_" + name] = ((grads[name][0] // 4, grads[name][1]), BF16)
-    scratch.update(sm=((8, D), F32), smr=((3, 8, D), F32), smz=((4, 8, D), F32))
-    copies = 96
+    for kind, count, names in (
+        ("g_", 8, GRADS), ("f_", 8, BY_SLOT), ("i_", 8, BY_SLOT), ("r_", 7, GRADS), ("p_", 1, GRADS)
+    ):
+        for name in names:
+            scratch[kind + name] = ((count,) + parts[name], BF16)
+    scratch.update(sm=((8, D), F32), smr=((5, 8, D), F32))
+    copies = 112
     shapes = [pltpu.VMEM(*one) for one in scratch.values()]
     shapes += [pltpu.SemaphoreType.DMA((copies,)) for _ in range(2)]
     shapes += [pltpu.SemaphoreType.DMA((24,))]
@@ -764,7 +838,7 @@
     )
     out = dict(zip(outs, results))
 
-    wide = {name: out["o_" + name].astype(F32) for name in order}
+    wide = {name: out["o_" + name].astype(F32) for name in GRADS}
     small = out["o_small"]
     bit = NEAR
     while bit < dp:
@@ -777,7 +851,14 @@
     def rows_of(name):
         return wide[name].reshape(-1, wide[name].shape[-1])
 
-    project_out_grad = jnp.moveaxis(wide["pout"], 0, 1).reshape(out_rows, D)
+    def side_by_side(part, blocks):
+        count, rows, columns = part.shape
+        part = part.reshape(blocks, count // blocks * rows, columns)
+        return jnp.moveaxis(part, 0, 1).reshape(-1, blocks * columns)
+
+    pin = jnp.concatenate([wide["pin0"], wide["pin1"], wide["pin2"]], axis=0)
+    project_in_grad = side_by_side(pin, 6).T
+    project_out_grad = side_by_side(wide["pout"], 2)
     return (
         out["block_out"],
         out["features_grad"],
@@ -787,7 +868,7 @@
         rows_of("embed"),
         small[0],
         small[1],
-        rows_of("pin"),
+        project_in_grad,
         project_out_grad,
         small[2],
         small[3],

time: 243 us -> 208 us (0.86); the launches traced: 239 us -> 208 us
  Pallas kernels: 224 us -> 191 us
    pallas_call x1, Pallas kernels: 224 us -> 191 us  [body(): pl.pallas_call(functools.partial(kernel, tuple(in_specs), tuple(outs), na...]
    unnamed x18 -> x17, local copies, waits for them, and re-layouts: 5.95 us -> 3.51 us
    reshape x4 -> x3, other arithmetic: 6.5 us -> 5.9 us  [rows_of(): return wide[name].reshape(-1, wide[name].shape[-1])]
where the time goes in v2:
time: 208 us
  Pallas kernels  191 us (92%)
  other arithmetic  8.5 us (4%)
  local copies, waits for them, and re-layouts  7.41 us (4%)
    pallas_call x1, Pallas kernels, body(): pl.pallas_call(functools.partial(kernel, tuple(in_specs), tuple(outs), na...  191 us
    reshape x3, other arithmetic, rows_of(): return wide[name].reshape(-1, wide[name].shape[-1])  5.9 us

profile of v2, /device:TPU:0, one launch (start us, length us, event | category | flops | bytes accessed | tf_op | source)
XLA Modules:
  0.0 207.6 jit_solution(8391782851180042358)
XLA Ops:
  0.7 190.9 %layer.1 = (bf16[288,768]{1,0:T(8,128)(2,1)}, f32[288,1024]{1,0:T(8,128)}, f32[8,768]{1,0:T(8,128)}, bf16[8,96,768]{2,1,0:T(8,128)(2,1)}, bf16[8,96,768]{2,1,0:T...) custom-call(bf16[1152,1024]{1,0:T(8,128)(2,1)} %refs_0_.1, ...), custom_call_target="tpu_custom_call" | custom-call | tf_op jit(solution)/shard_map/layer/pallas_call | solution.py:824
  191.6 1.2 pad_maximum_fusion
  192.8 1.3 bitcast_convert_fusion.2
  194.2 1.8 copy.34
  196.0 0.0 copy-start
  196.0 1.7 copy.36
  197.7 0.0 copy-done
  197.7 0.0 copy-start.6
  197.7 0.0 copy-start.5
  197.7 3.9 %bitcast_convert_fusion = (f32[768,768]{1,0:T(8,128)}, f32[768,768]{1,0:T(8,128)}) fusion(bf16[8,96,768]{2,1,0:T(8,128)(2,1)} %get-tuple-element.36, bf16[8,96,768]{2,1,0:T(8,128)(2,1)S(1)} %copy-done), kind=kLoop, calls=%fused_computation | loop fusion | flops 1179648 | bytes 7077888 | tf_op jit(solution)/shard_map/reshape | solution.py:852
  201.6 0.0 copy-start.2
  201.6 0.0 copy-done.6
  201.6 0.6 slice_reduce_fusion
  202.2 0.6 fusion
  202.8 0.0 copy-done.5
  202.8 0.0 copy-start.4
  202.9 0.0 copy-start.3
  202.9 0.9 copy.37
  203.7 0.0 copy-done.2
  203.7 0.0 copy-start.1
  203.7 1.1 bitcast_convert_fusion.3
  204.8 0.0 copy-done.4
  204.8 1.0 bitcast_convert_fusion.4
  205.8 0.0 copy-done.3
  205.8 0.8 copy.40
  206.5 0.0 copy-done.1
  206.5 1.0 copy.41
  (1 shorter events, 0.0 us)
Async XLA Ops:
  196.0 1.7 copy-start
  197.7 3.9 %copy-start.6 = (f32[8,768]{1,0:T(8,128)S(1)}, f32[8,768]{1,0:T(8,128)}, u32[]{:S(2)}) copy-start(f32[8,768]{1,0:T(8,128)} %get-tuple-element.29) | copy-start | bytes 73732
  197.7 5.1 %copy-start.5 = (bf16[8,48,384]{2,1,0:T(8,128)(2,1)S(1)}, bf16[8,48,384]{2,1,0:T(8,128)(2,1)}, u32[]{:S(2)}) copy-start(bf16[8,48,384]{2,1,0:T(8,128)(2,1)} %get-tuple-element.34) | copy-start | bytes 884740
  201.6 2.1 %copy-start.2 = (bf16[8,128,256]{2,1,0:T(8,128)(2,1)S(1)}, bf16[8,128,256]{2,1,0:T(8,128)(2,1)}, u32[]{:S(2)}) copy-start(bf16[8,128,256]{2,1,0:T(8,128)(2,1)} %get-tuple-element.28) | copy-start | bytes 1572868
  202.8 2.0 copy-start.4
  202.9 2.9 %copy-start.3 = (bf16[288,768]{1,0:T(8,128)(2,1)S(1)}, bf16[288,768]{1,0:T(8,128)(2,1)}, u32[]{:S(2)}) copy-start(bf16[288,768]{1,0:T(8,128)(2,1)} %get-tuple-element.76) | copy-start | bytes 1327108
  203.7 2.8 %copy-start.1 = (f32[288,1024]{1,0:T(8,128)S(1)}, f32[288,1024]{1,0:T(8,128)}, u32[]{:S(2)}) copy-start(f32[288,1024]{1,0:T(8,128)} %get-tuple-element.77) | copy-start | bytes 3538948

commit v3 on v2

--- a/solution.py
+++ b/solution.py
@@ -1,4 +1,5 @@
 import functools
+import itertools
 
 import jax
 import jax.numpy as jnp
@@ -65,71 +66,69 @@
 
 
 class Summed:
-    def __init__(self, net, place, order, grad, arrive, piece, out, far=None, far_in=None):
-        self.net, self.place, self.order = net, place, order
+    def __init__(self, net, place, away, back, grad, arrive, piece, out):
+        self.net, self.place, self.away, self.back = net, place, away, back
         self.grad, self.arrive, self.piece, self.out = grad, arrive, piece, out
-        self.far, self.far_in = far, far_in
-        self.at, self.size, self.slot = 0, grad.shape[0], 0
-        self.level, self.back = 0, False
-
-    def send_far(self):
-        self.copy = self.net.send(self.far, self.far_in, self.place.far)
-
-    def add(self, at, source, count):
-        for t in range(count):
-            self.grad[at + t] = (
-                self.grad[at + t].astype(F32) + source(t).astype(F32)
-            ).astype(BF16)
+        self.dims = "xyab"[4 - (len(grad.shape) - 2) :]
+        self.fixed = {}
+        self.level, self.gathered = 0, None
+
+    def index(self, dims, **more):
+        fixed = {**self.fixed, **more}
+        return tuple(pl.ds(fixed[dim], 1) if dim in fixed else pl.ds(0, 2) for dim in dims)
 
     def start(self):
-        bit, partner = self.place.partner(self.order[self.level])
-        half = self.size // 2
-        give = pl.ds(self.at + (1 - bit) * half, half)
-        self.at = self.at + bit * half
-        self.copy = self.net.send(
-            self.grad.at[give], self.arrive.at[pl.ds(self.slot, half)], partner
-        )
-
-    def share(self):
-        held = pl.ds(self.at, self.size)
-        bit, partner = self.place.partner(self.order[self.level])
-        self.copy = self.net.send(self.out.at[held], self.out.at[held], partner)
-        self.at = self.at - bit * self.size
+        dim = self.away[self.level]
+        bit, partner = self.place.partner(dim)
+        give = self.index(self.dims, **{dim: 1 - bit})
+        self.fixed[dim] = bit
+        self.copy = self.net.send(self.grad.at[give], self.arrive[self.level], partner)
+
+    def share(self, source):
+        dim = self.back[len(self.gathered)]
+        bit, partner = self.place.partner(dim)
+        held = self.index("yab")
+        self.copy = self.net.send(self.out.at[held] if source is None else source, self.out.at[held], partner)
+        self.gathered.append(dim)
+        del self.fixed[dim]
+
+    def add(self, arrived, store):
+        for at in itertools.product((0, 1), repeat=len(self.dims)):
+            here = dict(zip(self.dims, at))
+            if any(here[dim] for dim in self.fixed):
+                continue
+            where = tuple(self.fixed.get(dim, here[dim]) for dim in self.dims)
+            store(where, self.grad[where].astype(F32) + arrived[at].astype(F32))
 
     def step(self):
         self.copy.wait_recv()
-        if self.far is not None:
-            self.far = None
-            self.add(0, lambda t: self.far_in[t], self.size)
-            self.start()
-        elif not self.back:
-            half = self.size // 2
-            slot = self.slot
-            self.size, self.slot = half, slot + half
+        if self.gathered is None:
+            arrived = self.arrive[self.level]
             self.level += 1
-            if self.level < len(self.order):
-                self.add(self.at, lambda t: self.arrive[slot + t], half)
+            if self.level < len(self.away):
+
+                def store(where, value):
+                    self.grad[where] = value.astype(BF16)
+
+                self.add(arrived, store)
                 self.start()
             else:
-                self.back = True
-                self.level -= 1
-                self.piece[0] = (
-                    self.grad[self.at].astype(F32) + self.arrive[slot].astype(F32)
-                ).astype(BF16)
-                held = pl.ds(self.at, 1)
-                self.own = self.net.local(self.piece, self.out.at[held])
-                bit, partner = self.place.partner(self.order[self.level])
-                self.copy = self.net.send(self.piece, self.out.at[held], partner)
-                self.at = self.at - bit
+
+                def store(where, value):
+                    self.piece[0, 0, 0] = value.astype(BF16)
+
+                self.add(arrived, store)
+                self.fixed.pop("x", None)
+                self.gathered = []
+                self.own = self.net.local(self.piece, self.out.at[self.index("yab")])
+                self.share(self.piece)
         else:
-            if self.size == 1:
+            if len(self.gathered) == 1:
                 self.own.wait()
-            self.size *= 2
-            self.level -= 1
-            if self.level >= 0:
-                self.share()
-                return
-            self.copy = None
+            if len(self.gathered) < 3:
+                self.share(None)
+            else:
+                self.copy = None
 
     def step_all(self):
         while self.copy is not None:
@@ -144,7 +143,7 @@
         self.c = lax.rem(self.m, 2)
         self.y = lax.rem(self.d, 2)
         self.zi = lax.div(lax.rem(self.d, NEAR), 2)
-        self.bits = {"y": (self.y, 1), "a": (lax.rem(self.zi, 2), 2), "b": (lax.div(self.zi, 2), 4)}
+        self.bits = {"x": (0, None), "y": (self.y, 1), "a": (lax.rem(self.zi, 2), 2), "b": (lax.div(self.zi, 2), 4)}
         self.sib_m = self.m + 1 - 2 * self.c
         self.far_m = lax.rem(self.m + 2, 4)
         self.far_sib_m = lax.rem(self.sib_m + 2, 4)
@@ -154,20 +153,46 @@
 
     def partner(self, name):
         bit, stride = self.bits[name]
+        if stride is None:
+            return bit, self.far
         return bit, (self.d + stride - 2 * stride * bit, self.m)
 
 
-GRADS = ("up", "down", "pout", "pin0", "pin1", "pin2", "embed", "stem")
+GRADS = ("up", "down", "pout", "pin0", "pin1", "pin2", "embed", "stem0", "stem1")
 BY_SLOT = GRADS[2:]
-KINDS = dict(g="grad", f="far", i="far_in", r="arrive", p="piece", o="out")
+KINDS = dict(g="grad", p="piece", o="out", r0="arrive0", r1="arrive1", r2="arrive2", r3="arrive3")
+AWAY = dict(
+    down="yab",
+    up="bay",
+    pout="yxab",
+    pin0="yxab",
+    pin1="xyab",
+    pin2="xyba",
+    embed="xyab",
+    stem0="yxab",
+    stem1="xyab",
+)
+BACK = dict(
+    down="bay",
+    up="bay",
+    pout="aby",
+    pin0="aby",
+    pin1="bya",
+    pin2="yba",
+    embed="yba",
+    stem0="yab",
+    stem1="aby",
+)
 ORDER = (
-    "norm2", "mixed_back", "heads_far", "down", "up", "heads_own", "norm1_send", "down", "up",
-    "norm1", "pout", "stem_far", "stem_own", "down", "up", "features_send", "pin0", "pout",
-    "features_sum", "small", "result", "down", "up", "pout", "pin0", "embed", "small", "down",
-    "up", "pin0", "pout", "embed", "small", "stem", "pout", "pin0", "embed", "small", "stem",
-    "pout", "pin0", "pin1", "small", "embed", "stem", "pin0", "pin1", "pin2", "embed", "stem",
-    "pin1", "pin2", "embed", "stem", "pin1", "pin2", "stem", "pin1", "pin2", "stem", "pin1",
-    "pin2", "pin1", "pin2",
+    "norm2", "+result", "mixed_back", "+pout", "heads_far", "+pin1", "down", "heads_own", "pout",
+    "norm1_send", "+pin2", "norm1", "down", "pin1", "stem_far", "+pin0", "up", "pout",
+    "stem_own", "+embed", "pin1", "features_send", "small", "pin2", "down", "features_sum",
+    "+stem0", "+stem1", "result", "pin0", "up", "pout", "pin2", "pin1", "embed", "small", "down",
+    "pout", "stem0", "stem1", "pin2", "up", "pin1", "pin0", "embed", "small", "down", "stem0",
+    "pout", "pin2", "stem1", "up", "pin0", "pin1", "embed", "small", "pout", "stem0", "pin0",
+    "stem1", "embed", "down", "small", "pin2", "stem0", "pin1", "stem1", "up", "pout", "embed",
+    "stem0", "pin2", "pin0", "pin1", "embed", "stem1", "pin0", "stem0", "up", "pin2", "stem1",
+    "pin0", "embed", "stem1", "stem0",
 )
 
 
@@ -179,6 +204,8 @@
         kind, _, which = name.partition("_")
         if which in sums and kind in KINDS:
             sums[which][KINDS[kind]] = r.pop(name)
+    for refs in sums.values():
+        refs["arrive"] = [refs.pop(kind) for kind in sorted(refs) if kind.startswith("arrive")]
     run(sums=sums, **r)
 
 
@@ -205,7 +232,7 @@
         return pl.ds(pl.multiple_of(m * R, 16), R)
 
     barrier = pltpu.get_barrier_semaphore()
-    peers = [place.sib, place.far] + [place.partner(name)[1] for name in place.bits]
+    peers = [place.sib] + [place.partner(name)[1] for name in place.bits]
     for peer in peers:
         pl.semaphore_signal(barrier, inc=1, device_id=peer, device_id_type=MESH)
     l_stem = net.local(stem_weight, stem.at[0])
@@ -484,27 +511,26 @@
     sbuf[:, 0:D] = out_part(place.far_m)
     c_core[0, 1].wait_recv()
     xsend[0] = (sbuf[:, 0:D] + crecv[0, 1].astype(F32)).astype(BF16)
-    c_far[0] = net.send(xsend.at[0], xrecv.at[0], place.far)
-
-    def make(name, order):
-        return Summed(net, place, order, **sums[name])
-
-    summed = {name: make(name, "ayb" if name == "up" else "yab") for name in GRADS}
-
-    def keep(name, which, at, value):
-        ref = sums[name][which]
-        rows = ref.shape[1]
-        count = value.shape[0] // rows
-        ref[at : at + count] = value.reshape(count, rows, value.shape[1]).astype(BF16)
+
+    summed = {name: Summed(net, place, AWAY[name], BACK[name], **sums[name]) for name in GRADS}
+
+    def keep(name, slot, at, value):
+        ref = sums[name]["grad"]
+        rows = ref.shape[-2]
+        for t in range(value.shape[0] // rows):
+            part = (at + t) // 4, (at + t) // 2 % 2, (at + t) % 2
+            ref[part if slot is None else (slot,) + part] = value[
+                t * rows : (t + 1) * rows
+            ].astype(BF16)
 
     half = D // 2
     for i in range(2):
         value = dot(hid[:, i * half : (i + 1) * half], branch[...], 0, 0)
-        keep("down", "grad", 4 * i, value)
+        keep("down", None, 4 * i, value)
     summed["down"].start()
     for i in range(2):
         value = dot(n2[:, i * half : (i + 1) * half], preg[...], 0, 0)
-        keep("up", "grad", 4 * i, value)
+        keep("up", None, 4 * i, value)
     summed["up"].start()
     sm[...] = jnp.zeros_like(sm)
     sm[4:5, :] = bias_sum[0] + bias_sum[1] + bias_sum[2] + bias_sum[3]
@@ -574,11 +600,10 @@
         copies["mb"].wait_recv()
         value = dot(mixed[...], mb[...], 0, 0)
         shard = pout.shape[1]
-        for j, which in ((1, "far"), (0, "grad")):
+        for j in range(2):
             rows = value[j * shard : (j + 1) * shard]
             for i in range(2):
-                keep("pout", which, 4 * i, rows[:, i * half : (i + 1) * half])
-        summed["pout"].send_far()
+                keep("pout", j, 4 * i, rows[:, i * half : (i + 1) * half])
         for at, size in tile_rows:
             value = dot(mb[at : at + size, :], whole_out, 1, 1).astype(BF16)
             for h in range(2 * per_shard):
@@ -595,7 +620,7 @@
         q[h] = dq
         return carry
 
-    def pin_back(j, which):
+    def pin_back(j):
         lax.fori_loop(per_shard * j, per_shard * (j + 1), head_back, 0)
 
         def store_pg(lanes, value):
@@ -606,16 +631,15 @@
         value = dot(pg[j], n1[...], 0, 0)
         wide = D // 6
         for i in range(6):
-            keep("pin%d" % (i // 2), which, 4 * (i % 2), value[:, i * wide : (i + 1) * wide])
+            keep("pin%d" % (i // 2), j, 4 * (i % 2), value[:, i * wide : (i + 1) * wide])
 
     @task
     def heads_far():
-        pin_back(1, "far")
-        summed["pin0"].send_far()
+        pin_back(1)
 
     @task
     def heads_own():
-        pin_back(0, "grad")
+        pin_back(0)
 
     @task
     def norm1_send():
@@ -640,12 +664,12 @@
         norm_back(grad_of, first_gain, xh1, rs1, None, eb, own_rows, 0)
         copies["eb"] = net.send(eb.at[own_part], eb.at[own_part], place.sib)
 
-    def embed_back(j, which):
-        keep("embed", which, 0, dot(act[j], eb[...], 0, 0))
+    def embed_back(j):
+        keep("embed", j, 0, dot(act[j], eb[...], 0, 0))
 
     cin = feat.shape[1]
 
-    def stem_back(j, which):
+    def stem_back(j):
         gain_sum = jnp.zeros((1, channels), F32)
         bias_total = jnp.zeros((1, channels), F32)
         for at, size in tile_rows:
@@ -680,21 +704,21 @@
         for t in range(4):
             rows = slice(t * quarter, (t + 1) * quarter)
             xh = (stem[j, rows, :].astype(F32) - average) * scale
-            keep("stem", which, 2 * t, (gtmp[rows, :] - sum_one - xh * sum_two) * scale)
+            value = (gtmp[rows, :] - sum_one - xh * sum_two) * scale
+            for i in range(2):
+                lanes = slice(i * channels // 2, (i + 1) * channels // 2)
+                keep("stem%d" % i, j, 2 * t, value[:, lanes])
 
     @task
     def stem_far():
         copies["eb"].wait_recv()
-        embed_back(1, "far")
-        summed["embed"].send_far()
-        stem_back(1, "far")
-        for name in ("stem", "pin1", "pin2"):
-            summed[name].send_far()
+        embed_back(1)
+        stem_back(1)
 
     @task
     def stem_own():
-        embed_back(0, "grad")
-        stem_back(0, "grad")
+        embed_back(0)
+        stem_back(0)
         small("core")
 
     @task
@@ -714,7 +738,7 @@
         sbuf[...] = copies["feat_own"] + rbuf[...]
         locals_left.append(net.local(sbuf, features_grad))
 
-    small_at = {"core": place.sib, "x": place.far}
+    small_at = {"core": place.sib}
     for name in place.bits:
         small_at[name] = place.partner(name)[1]
     small_order = tuple(small_at)
@@ -740,6 +764,10 @@
     for name in ORDER:
         if name in tasks:
             tasks.pop(name)()
+        elif name == "+result":
+            c_far[0] = net.send(xsend.at[0], xrecv.at[0], place.far)
+        elif name[0] == "+":
+            summed[name[1:]].start()
         elif name == "small":
             small_step(small_next.pop(0))
         else:
@@ -750,6 +778,58 @@
     for copy in locals_left:
         copy.wait()
     net.finish()
+
+
+def finish(in_names, out_names, *refs):
+    names = in_names + out_names
+    r = dict(zip(names, refs))
+    rest = refs[len(names) :]
+    sems, passed, rest = rest[0], rest[1:3], rest[3:]
+    held, made = rest[: len(GRADS)], rest[len(GRADS) :]
+    made = dict(zip(("up", "down", "pout", "pin", "embed", "stem"), made))
+    count = [0]
+    going = []
+
+    def move(src, dst):
+        copy = pltpu.make_async_copy(src, dst, sems.at[count[0]])
+        count[0] += 1
+        copy.start()
+        return copy
+
+    order = ("up", "down", "stem0", "stem1", "embed", "pin0", "pin1", "pin2", "pout")
+    held = dict(zip(GRADS, held))
+    as_is = ("block_out", "features_grad")
+    passing = [move(r["i_" + name], ref) for name, ref in zip(as_is, passed)]
+    arriving = {name: move(r["i_" + name], held[name]) for name in order}
+    small = r["i_small"]
+    for i, name in enumerate(("g1", "b1", "g2", "b2", "ub")):
+        r["o_" + name][...] = small[i, :]
+    channels = r["o_gain"].shape[0]
+    r["o_gain"][...] = small[5, 0:channels]
+    r["o_shift"][...] = small[5, channels : 2 * channels]
+    for name, ref, copy in zip(as_is, passed, passing):
+        copy.wait()
+        going.append(move(ref, r["o_" + name]))
+    for name in order:
+        arriving[name].wait()
+        part = held[name]
+        rows, columns = part.shape[1:]
+        whole = name.rstrip("012")
+        down = made[whole].shape[0] // rows
+        for t in range(8):
+            at = slice(t % down * rows, (t % down + 1) * rows)
+            left = t // down * columns
+            if whole in ("pin", "stem"):
+                left += int(name[-1]) * made[whole].shape[1] // dict(pin=3, stem=2)[whole]
+            made[whole][at, left : left + columns] = part[t].astype(F32)
+            last = name not in ("pin0", "pin1", "stem0")
+            if last and (t == 3 or t == 7) and whole in ("up", "down"):
+                half = pl.ds(t // 4 * 4 * rows, 4 * rows)
+                going.append(move(made[whole].at[half], r["o_" + whole].at[half]))
+            elif last and t == 7:
+                going.append(move(made[whole], r["o_" + whole]))
+    for copy in going:
+        copy.wait()
 
 
 def body(
@@ -784,7 +864,8 @@
         pin1=(wide_in // 4, D // 6),
         pin2=(wide_in // 4, D // 6),
         embed=(channels // 8, D),
-        stem=(cin // 8, channels),
+        stem0=(cin // 8, channels // 2),
+        stem1=(cin // 8, channels // 2),
     )
     outs = dict(
         block_out=((R, D), BF16, hbm),
@@ -792,7 +873,7 @@
         o_small=((8, D), F32, vmem),
     )
     for name in GRADS:
-        outs["o_" + name] = ((8,) + parts[name], BF16, hbm)
+        outs["o_" + name] = ((2, 2, 2) + parts[name], BF16, hbm)
     scratch = dict(
         feat=((L, cin), BF16), stem=((2, cin, channels), BF16), std=((2, cin, channels), BF16),
         wstat=((2, 8, channels), F32), embed=((2, channels, D), BF16), pin=((2, wide_in, D), BF16),
@@ -810,13 +891,15 @@
         mb=((L, D), BF16), pg=((2, L, wide_in), BF16),
         sg=((2, L, channels), BF16), gtmp=((cin, channels), F32),
     )
-    for kind, count, names in (
-        ("g_", 8, GRADS), ("f_", 8, BY_SLOT), ("i_", 8, BY_SLOT), ("r_", 7, GRADS), ("p_", 1, GRADS)
-    ):
-        for name in names:
-            scratch[kind + name] = ((count,) + parts[name], BF16)
+    for name in GRADS:
+        size = dict.fromkeys(sorted(AWAY[name], key="xyab".index), 2)
+        scratch["g_" + name] = (tuple(size.values()) + parts[name], BF16)
+        for level, dim in enumerate(AWAY[name]):
+            size[dim] = 1
+            scratch["r%d_" % level + name] = (tuple(size.values()) + parts[name], BF16)
+        scratch["p_" + name] = ((1, 1, 1) + parts[name], BF16)
     scratch.update(sm=((8, D), F32), smr=((5, 8, D), F32))
-    copies = 112
+    copies = 128
     shapes = [pltpu.VMEM(*one) for one in scratch.values()]
     shapes += [pltpu.SemaphoreType.DMA((copies,)) for _ in range(2)]
     shapes += [pltpu.SemaphoreType.DMA((24,))]
@@ -838,9 +921,11 @@
     )
     out = dict(zip(outs, results))
 
-    wide = {name: out["o_" + name].astype(F32) for name in GRADS}
+    wide = {name: out["o_" + name].reshape((8,) + parts[name]) for name in GRADS}
     small = out["o_small"]
     bit = NEAR
+    if bit < dp:
+        wide = {name: part.astype(F32) for name, part in wide.items()}
     while bit < dp:
         pairs = [(i, i ^ bit) for i in range(dp)]
         wide, small = jax.tree.map(
@@ -848,33 +933,49 @@
         )
         bit *= 2
 
-    def rows_of(name):
-        return wide[name].reshape(-1, wide[name].shape[-1])
-
-    def side_by_side(part, blocks):
-        count, rows, columns = part.shape
-        part = part.reshape(blocks, count // blocks * rows, columns)
-        return jnp.moveaxis(part, 0, 1).reshape(-1, blocks * columns)
-
-    pin = jnp.concatenate([wide["pin0"], wide["pin1"], wide["pin2"]], axis=0)
-    project_in_grad = side_by_side(pin, 6).T
-    project_out_grad = side_by_side(wide["pout"], 2)
+    inputs = {"i_" + name: wide[name] for name in GRADS}
+    inputs.update(i_block_out=out["block_out"], i_features_grad=out["features_grad"], i_small=small)
+    whole = dict(
+        up=(D, hidden), down=(hidden, D), pout=(out_rows, D), pin=(wide_in, D),
+        embed=(channels, D), stem=(cin, channels),
+    )
+    finals = dict(o_block_out=((R, D), BF16, hbm), o_features_grad=((R, cin), F32, hbm))
+    for name, shape in whole.items():
+        finals["o_" + name] = (shape, F32, hbm)
+    for name in ("g1", "b1", "g2", "b2"):
+        finals["o_" + name] = ((D,), F32, vmem)
+    finals["o_ub"] = ((hidden,), F32, vmem)
+    for name in ("gain", "shift"):
+        finals["o_" + name] = ((channels,), F32, vmem)
+    moved = pl.pallas_call(
+        functools.partial(finish, tuple(inputs), tuple(finals)),
+        out_shape=[jax.ShapeDtypeStruct(shape, kind) for shape, kind, _ in finals.values()],
+        in_specs=[hbm] * (len(inputs) - 1) + [vmem],
+        out_specs=[spec for _, _, spec in finals.values()],
+        scratch_shapes=[pltpu.SemaphoreType.DMA((24,))]
+        + [pltpu.VMEM((R, D), BF16), pltpu.VMEM((R, cin), F32)]
+        + [pltpu.VMEM(wide[name].shape, wide[name].dtype) for name in GRADS]
+        + [pltpu.VMEM(shape, F32) for shape in whole.values()],
+        compiler_params=pltpu.CompilerParams(vmem_limit_bytes=62 * 2**20),
+        name="finish",
+    )(*inputs.values())
+    done = dict(zip(finals, moved))
     return (
-        out["block_out"],
-        out["features_grad"],
-        rows_of("stem"),
-        small[5, 0:channels],
-        small[5, channels : 2 * channels],
-        rows_of("embed"),
-        small[0],
-        small[1],
-        project_in_grad,
-        project_out_grad,
-        small[2],
-        small[3],
-        rows_of("up"),
-        small[4],
-        rows_of("down"),
+        done["o_block_out"],
+        done["o_features_grad"],
+        done["o_stem"],
+        done["o_gain"],
+        done["o_shift"],
+        done["o_embed"],
+        done["o_g1"],
+        done["o_b1"],
+        done["o_pin"].T,
+        done["o_pout"],
+        done["o_g2"],
+        done["o_b2"],
+        done["o_up"],
+        done["o_ub"],
+        done["o_down"],
     )
 
 

time: 208 us -> 193 us (0.928)
  other arithmetic: 8.5 us -> 0 us
  local copies, waits for them, and re-layouts: 7.41 us -> 0 us
    pallas_call x0 -> x1, Pallas kernels: none -> 6.88 us  [body(): pl.pallas_call(functools.partial(finish, tuple(inputs), tuple(finals)), o...]
    reshape x3 -> x0, other arithmetic: 5.9 us -> none  [rows_of(): return wide[name].reshape(-1, wide[name].shape[-1])]
    pallas_call x1, Pallas kernels: 191 us -> 185 us  [body(): pl.pallas_call(functools.partial(kernel, tuple(in_specs), tuple(outs), na...]
    unnamed x17 -> x0, local copies, waits for them, and re-layouts: 3.51 us -> none
where the time goes in v3:
time: 193 us
  Pallas kernels  192 us (99%)
    pallas_call x1, Pallas kernels, body(): pl.pallas_call(functools.partial(kernel, tuple(in_specs), tuple(outs), na...  185 us
    pallas_call x1, Pallas kernels, body(): pl.pallas_call(functools.partial(finish, tuple(inputs), tuple(finals)), o...  6.88 us

profile of v3, /device:TPU:0, one launch (start us, length us, event | category | flops | bytes accessed | tf_op | source)
XLA Modules:
  0.0 192.9 jit_solution(9150577139245260822)
XLA Ops:
  0.7 185.2 %layer.1 = (bf16[288,768]{1,0:T(8,128)(2,1)}, f32[288,1024]{1,0:T(8,128)}, f32[8,768]{1,0:T(8,128)}, bf16[2,2,2,96,768]{4,3,2,1,0:T(8,128)(2,1)}, bf16[2,2,2,96,...) custom-call(bf16[1152,1024]{1,0:T(8,128)(2,1)} %refs_0_.1, ...), custom_call_target="tpu_custom_call" | custom-call | tf_op jit(solution)/shard_map/layer/pallas_call | solution.py:907
  185.9 6.9 %finish.1 = (bf16[288,768]{1,0:T(8,128)(2,1)}, f32[288,1024]{1,0:T(8,128)}, f32[768,768]{1,0:T(8,128)}, f32[768,768]{1,0:T(8,128)}, f32[192,768]{1,0:T(8,128)}, ...) custom-call(bf16[8,96,768]{2,1,0:T(8,128)(2,1)} %bitcast.11, ...), custom_call_target="tpu_custom_call" | custom-call | tf_op jit(solution)/shard_map/finish/pallas_call | solution.py:950
